TPU v7x, 32 devices: a whole 2x2x4 slice. The times are simulated.
32 devices in a mesh: dp: 8 (over z, x), blk: 4 (over y, core).
Axes of the slice: x: 2, y: 2, z: 4, core: 2. Of those that a mesh axis runs over, the one named last changes fastest.
Arguments:
- tokens: bfloat16 [2, 8, 512, 768], P(None, 'dp', 'blk'), may hold values from -6 to 6
- timesteps: int32 [2, 8], P(None, 'dp'), may hold values from 0 to 999
- routes: int32 [2, 8, 512, 2], P(None, 'dp', 'blk'), may hold values from 0 to 3, all different within a row; in each aligned block of 128 rows (0 to 127, 128 to 255, ..., all dimensions but the last counted through in order) at most 68 rows name the same one
- ada_weight: bfloat16 [768, 4608], P('dp', 'blk'), may hold values from -0.3125 to 0.3125
- qkv_weight: bfloat16 [768, 2304], P('dp', 'blk'), may hold values from -0.21875 to 0.21875
- out_weight: bfloat16 [768, 768], P('dp', 'blk'), may hold values from -0.3125 to 0.3125
- router_weight: bfloat16 [768, 4], P('dp', 'blk'), may hold values from -0.109375 to 0.109375
- shared_in_weight: bfloat16 [768, 3072], P('dp', 'blk'), may hold values from -0.21875 to 0.21875
- shared_out_weight: bfloat16 [3072, 768], P('blk', 'dp'), may hold values from -0.109375 to 0.109375
- expert_in_weight: bfloat16 [4, 768, 3072], P('blk', 'dp'), may hold values from -0.21875 to 0.21875
- expert_out_weight: bfloat16 [4, 3072, 768], P('blk', None, 'dp'), may hold values from -0.109375 to 0.109375
- cotangent: bfloat16 [2, 8, 512, 768], P(None, 'dp', 'blk'), may hold values from -6 to 6
Outputs:
- block_out: bfloat16 [2, 8, 512, 768], P(None, 'dp', 'blk')
- tokens_grad: float32 [2, 8, 512, 768], P(None, 'dp', 'blk')
- ada_grad: float32 [768, 4608], P('dp', 'blk')
- qkv_grad: float32 [768, 2304], P('dp', 'blk')
- out_grad: float32 [768, 768], P('dp', 'blk')
- router_grad: float32 [768, 4], P('dp', 'blk')
- shared_in_grad: float32 [768, 3072], P('dp', 'blk')
- shared_out_grad: float32 [3072, 768], P('blk', 'dp')
- expert_in_grad: float32 [4, 768, 3072], P('blk', 'dp')
- expert_out_grad: float32 [4, 3072, 768], P('blk', None, 'dp')
Inputs may be any that keep to these rules, and one draw needn't show every extreme that they name: `routes`: each row names 2 different experts. In every aligned block of 128 rows (the patches of one device in one micro-batch) no expert is named more than 68 times, and in every draw some block names some expert exactly 68 times.
All inputs are finite; a program needn't handle non-finite values.
Results may differ from a plain program's by a relative error of at most 0.017.
Values may be sent and summed in bfloat16 or wider, within the bound.
No kernel may reach another device: no remote copies, remote signals or barrier semaphores. Data moves between devices by JAX's collectives and lax.ppermute only.
A program may use at most 256 MiB of HBM per device.

v0:
```python
import math

import jax
import jax.numpy as jnp
from jax import lax
from jax.sharding import PartitionSpec as P

D = 768
HEADS = 12
HEAD_DIM = 64
EXP_DEV = 1
TOP = 2


eps_norm = 1e-06


def modulate(row_values, row_shift, row_scale):
    row_mean = jnp.mean(row_values, axis=-1, keepdims=True)
    centered = row_values - row_mean
    row_var = jnp.mean(centered * centered, axis=-1, keepdims=True)
    return centered * lax.rsqrt(row_var + eps_norm) * (1.0 + row_scale) + row_shift


def timestep_features(step_index, feature_width):
    half_width = feature_width // 2
    frequency = jnp.exp(-math.log(10000.0) * jnp.arange(half_width, dtype=jnp.float32) / half_width)
    angles = step_index.astype(jnp.float32) * frequency
    return jnp.concatenate([jnp.cos(angles), jnp.sin(angles)])


def gelu_tanh(values_in):
    return jax.nn.gelu(values_in, approximate=True)


def slot_tables(routing, experts, capacity):
    flat_ids = routing.reshape(-1)
    pair_count = flat_ids.shape[0]
    onehot = (flat_ids[:, None] == jnp.arange(experts, dtype=jnp.int32)[None, :]).astype(jnp.int32)
    before = jnp.cumsum(onehot, axis=0) - onehot
    position = jnp.sum(before * onehot, axis=1)
    slot_index = flat_ids * capacity + position
    sources = (
        jnp.full((experts * capacity,), pair_count, jnp.int32)
        .at[slot_index]
        .set(jnp.arange(pair_count, dtype=jnp.int32))
    )
    filled = sources < pair_count
    return (slot_index, jnp.minimum(sources, pair_count - 1), filled)


def head_groups(matrix):
    head_group = math.gcd(HEADS, 4)
    return matrix.reshape(matrix.shape[0], HEADS // head_group, head_group, HEAD_DIM).transpose(
        1, 0, 2, 3
    )


def ungroup(tensor):
    return tensor.transpose(1, 0, 2, 3).reshape(tensor.shape[1], D)


def attend_group(operands):
    query_part, key_part, value_part = operands
    score_scale = 1.0 / math.sqrt(HEAD_DIM)
    scores = (
        jnp.einsum("qhd,khd->hqk", query_part, key_part, preferred_element_type=jnp.float32)
        * score_scale
    )
    top_score = jnp.max(scores, axis=-1, keepdims=True)
    exp_scores = jnp.exp(scores - top_score)
    row_total = jnp.sum(exp_scores, axis=-1, keepdims=True)
    probs = (exp_scores / row_total).astype(jnp.bfloat16)
    mixed_heads = jnp.einsum("hqk,khd->qhd", probs, value_part, preferred_element_type=jnp.float32)
    return (mixed_heads.astype(jnp.bfloat16), top_score[..., 0] + jnp.log(row_total[..., 0]))


def attend_back(operands):
    query_part, key_part, value_part, grad_part, lse_part = operands
    score_scale = 1.0 / math.sqrt(HEAD_DIM)
    scores = (
        jnp.einsum("qhd,khd->hqk", query_part, key_part, preferred_element_type=jnp.float32)
        * score_scale
    )
    probs = jnp.exp(scores - lse_part[..., None])
    grad_probs = jnp.einsum(
        "qhd,khd->hqk", grad_part, value_part, preferred_element_type=jnp.float32
    )
    grad_scores = (
        probs * (grad_probs - jnp.sum(probs * grad_probs, axis=-1, keepdims=True))
    ).astype(jnp.bfloat16)
    grad_query = (
        jnp.einsum("hqk,khd->qhd", grad_scores, key_part, preferred_element_type=jnp.float32)
        * score_scale
    )
    grad_key = (
        jnp.einsum("hqk,qhd->khd", grad_scores, query_part, preferred_element_type=jnp.float32)
        * score_scale
    )
    grad_value = jnp.einsum(
        "hqk,qhd->khd", probs.astype(jnp.bfloat16), grad_part, preferred_element_type=jnp.float32
    )
    return (grad_query, grad_key, grad_value)


def fetch_weights(shards):
    wide_parts = (
        lax.all_gather(shards[0], "dp", axis=0, tiled=True),
        lax.all_gather(shards[1], "dp", axis=0, tiled=True),
        lax.all_gather(shards[2], "dp", axis=0, tiled=True),
        lax.all_gather(shards[3], "dp", axis=0, tiled=True),
        lax.all_gather(shards[4], "dp", axis=0, tiled=True),
        lax.all_gather(shards[5], "dp", axis=1, tiled=True),
        lax.all_gather(shards[6], "dp", axis=1, tiled=True),
        lax.all_gather(shards[7], "dp", axis=2, tiled=True),
    )
    dense_parts = (
        lax.all_gather(wide_parts[0], "blk", axis=1, tiled=True),
        lax.all_gather(wide_parts[1], "blk", axis=1, tiled=True),
        lax.all_gather(wide_parts[2], "blk", axis=1, tiled=True),
        lax.all_gather(wide_parts[3], "blk", axis=1, tiled=True),
        lax.all_gather(wide_parts[4], "blk", axis=1, tiled=True),
        lax.all_gather(wide_parts[5], "blk", axis=0, tiled=True),
    )
    return tuple(dense_parts) + (wide_parts[6], wide_parts[7])


def reduce_grads(grads):
    dense_parts = (
        lax.psum_scatter(
            grads[0].astype(jnp.bfloat16), "blk", scatter_dimension=1, tiled=True
        ).astype(jnp.float32),
        lax.psum_scatter(
            grads[1].astype(jnp.bfloat16), "blk", scatter_dimension=1, tiled=True
        ).astype(jnp.float32),
        lax.psum_scatter(
            grads[2].astype(jnp.bfloat16), "blk", scatter_dimension=1, tiled=True
        ).astype(jnp.float32),
        lax.psum_scatter(
            grads[3].astype(jnp.bfloat16), "blk", scatter_dimension=1, tiled=True
        ).astype(jnp.float32),
        lax.psum_scatter(
            grads[4].astype(jnp.bfloat16), "blk", scatter_dimension=1, tiled=True
        ).astype(jnp.float32),
        lax.psum_scatter(
            grads[5].astype(jnp.bfloat16), "blk", scatter_dimension=0, tiled=True
        ).astype(jnp.float32),
    )
    return tuple(
        (
            lax.psum_scatter(dense_parts[0], "dp", scatter_dimension=0, tiled=True),
            lax.psum_scatter(dense_parts[1], "dp", scatter_dimension=0, tiled=True),
            lax.psum_scatter(dense_parts[2], "dp", scatter_dimension=0, tiled=True),
            lax.psum_scatter(dense_parts[3], "dp", scatter_dimension=0, tiled=True),
            lax.psum_scatter(dense_parts[4], "dp", scatter_dimension=0, tiled=True),
            lax.psum_scatter(dense_parts[5], "dp", scatter_dimension=1, tiled=True),
            lax.psum_scatter(grads[6], "dp", scatter_dimension=1, tiled=True),
            lax.psum_scatter(grads[7], "dp", scatter_dimension=2, tiled=True),
        )
    )


def run_micro(weights, tokens_in, step_index, routing, cotangent_in):
    (
        ada_full,
        qkv_full,
        out_full,
        router_full,
        shared_in_full,
        shared_out_full,
        expert_in_full,
        expert_out_full,
    ) = weights
    blk_count = lax.axis_size("blk")
    row_count = tokens_in.shape[0]
    experts_all = EXP_DEV * blk_count
    capacity = row_count * TOP // experts_all + max(2, row_count // 32)
    cond_act = jax.nn.silu(timestep_features(step_index, D)).astype(jnp.bfloat16)
    modulation = jnp.dot(cond_act[None, :], ada_full, preferred_element_type=jnp.float32)[0]
    shift_one, scale_one, gate_one, shift_two, scale_two, gate_two = jnp.split(modulation, 6)
    tokens_f = tokens_in.astype(jnp.float32)
    normed_one_f, tokens_back = jax.vjp(modulate, tokens_f, shift_one, scale_one)
    normed_one = normed_one_f.astype(jnp.bfloat16)
    projected = jnp.dot(normed_one, qkv_full, preferred_element_type=jnp.float32).astype(
        jnp.bfloat16
    )
    queries, key_local, value_local = jnp.split(projected, 3, axis=1)
    key_all, value_all = (
        lax.all_gather(key_local, "blk", axis=0, tiled=True),
        lax.all_gather(value_local, "blk", axis=0, tiled=True),
    )
    query_groups = head_groups(queries)
    key_groups = head_groups(key_all)
    value_groups = head_groups(value_all)
    mixed_groups, lse_groups = lax.map(attend_group, (query_groups, key_groups, value_groups))
    mixed_heads = ungroup(mixed_groups)
    attended = jnp.dot(mixed_heads, out_full, preferred_element_type=jnp.float32)
    residual = tokens_f + gate_one * attended
    normed_two_f, residual_back = jax.vjp(modulate, residual, shift_two, scale_two)
    normed_two = normed_two_f.astype(jnp.bfloat16)
    logits = jnp.dot(normed_two, router_full, preferred_element_type=jnp.float32)
    gate_probs = jax.nn.softmax(jnp.take_along_axis(logits, routing, axis=1), axis=-1)
    shared_pre = jnp.dot(normed_two, shared_in_full, preferred_element_type=jnp.float32)
    shared_act_f, shared_back = jax.vjp(gelu_tanh, shared_pre)
    shared_act = shared_act_f.astype(jnp.bfloat16)
    shared_val = jnp.dot(shared_act, shared_out_full, preferred_element_type=jnp.float32)
    slot_index, sources, filled = slot_tables(routing, experts_all, capacity)
    send_rows = jnp.where(filled[:, None], normed_two[sources // TOP], jnp.zeros((), jnp.bfloat16))
    send_rows = send_rows.reshape(blk_count, EXP_DEV, capacity, D)
    arrived_rows = lax.all_to_all(send_rows, "blk", split_axis=0, concat_axis=0, tiled=True)
    pre_values = jnp.einsum(
        "sekd,edf->sekf", arrived_rows, expert_in_full, preferred_element_type=jnp.float32
    )
    act_values = gelu_tanh(pre_values).astype(jnp.bfloat16)
    result = jnp.einsum(
        "sekf,efd->sekd", act_values, expert_out_full, preferred_element_type=jnp.float32
    )
    expert_val = result.astype(jnp.bfloat16)
    returned = lax.all_to_all(expert_val, "blk", split_axis=0, concat_axis=0, tiled=True).reshape(
        -1, D
    )
    routed = returned[slot_index].reshape(row_count, TOP, D).astype(jnp.float32)
    mixture = shared_val + jnp.sum(gate_probs[:, :, None] * routed, axis=1)
    block_rows = (residual + gate_two * mixture).astype(jnp.bfloat16)
    grad_block = cotangent_in.astype(jnp.float32)
    grad_gate_two = jnp.sum(grad_block * mixture, axis=0)
    grad_mix = grad_block * gate_two
    grad_shared_val = grad_mix.astype(jnp.bfloat16)
    grad_gates = jnp.sum(grad_mix[:, None, :] * routed, axis=-1)
    grad_pairs = (
        (gate_probs[:, :, None] * grad_mix[:, None, :])
        .astype(jnp.bfloat16)
        .reshape(row_count * TOP, D)
    )
    send_grads = jnp.where(filled[:, None], grad_pairs[sources], jnp.zeros((), jnp.bfloat16))
    send_grads = send_grads.reshape(blk_count, EXP_DEV, capacity, D)
    arrived_grads = lax.all_to_all(send_grads, "blk", split_axis=0, concat_axis=0, tiled=True)
    expert_act_f, expert_back = jax.vjp(gelu_tanh, pre_values)
    expert_act = expert_act_f.astype(jnp.bfloat16)
    expert_out_grad = jnp.einsum(
        "sekf,sekd->efd", expert_act, arrived_grads, preferred_element_type=jnp.float32
    )
    grad_act = jnp.einsum(
        "sekd,efd->sekf", arrived_grads, expert_out_full, preferred_element_type=jnp.float32
    )
    grad_expert_pre = expert_back(grad_act)[0].astype(jnp.bfloat16)
    expert_in_grad = jnp.einsum(
        "sekd,sekf->edf", arrived_rows, grad_expert_pre, preferred_element_type=jnp.float32
    )
    grad_arrived = jnp.einsum(
        "sekf,edf->sekd", grad_expert_pre, expert_in_full, preferred_element_type=jnp.float32
    )
    grad_returned = (
        lax.all_to_all(
            grad_arrived.astype(jnp.bfloat16), "blk", split_axis=0, concat_axis=0, tiled=True
        )
        .astype(grad_arrived.dtype)
        .reshape(-1, D)
    )
    grad_normed_two = jnp.sum(grad_returned[slot_index].reshape(row_count, TOP, D), axis=1)
    shared_out_grad = jnp.dot(shared_act.T, grad_shared_val, preferred_element_type=jnp.float32)
    grad_shared_act = jnp.dot(
        grad_shared_val, shared_out_full.T, preferred_element_type=jnp.float32
    )
    grad_shared_pre = shared_back(grad_shared_act)[0].astype(jnp.bfloat16)
    shared_in_grad = jnp.dot(normed_two.T, grad_shared_pre, preferred_element_type=jnp.float32)
    grad_normed_two = grad_normed_two + jnp.dot(
        grad_shared_pre, shared_in_full.T, preferred_element_type=jnp.float32
    )
    grad_chosen = gate_probs * (
        grad_gates - jnp.sum(gate_probs * grad_gates, axis=-1, keepdims=True)
    )
    picked = (
        routing[:, :, None] == jnp.arange(experts_all, dtype=jnp.int32)[None, None, :]
    ).astype(jnp.float32)
    grad_logits = jnp.sum(picked * grad_chosen[:, :, None], axis=1).astype(jnp.bfloat16)
    router_grad = jnp.dot(normed_two.T, grad_logits, preferred_element_type=jnp.float32)
    grad_normed_two = grad_normed_two + jnp.dot(
        grad_logits, router_full.T, preferred_element_type=jnp.float32
    )
    grad_residual_norm, grad_shift_two, grad_scale_two = residual_back(grad_normed_two)
    grad_residual = grad_block + grad_residual_norm
    grad_gate_one = jnp.sum(grad_residual * attended, axis=0)
    grad_attended = (grad_residual * gate_one).astype(jnp.bfloat16)
    out_grad = jnp.dot(mixed_heads.T, grad_attended, preferred_element_type=jnp.float32)
    grad_mixed = jnp.dot(grad_attended, out_full.T, preferred_element_type=jnp.float32).astype(
        jnp.bfloat16
    )
    grad_query, grad_key, grad_value = lax.map(
        attend_back, (query_groups, key_groups, value_groups, head_groups(grad_mixed), lse_groups)
    )
    key_grads, value_grads = (
        lax.psum_scatter(
            ungroup(grad_key).astype(jnp.bfloat16), "blk", scatter_dimension=0, tiled=True
        ).astype(jnp.float32),
        lax.psum_scatter(
            ungroup(grad_value).astype(jnp.bfloat16), "blk", scatter_dimension=0, tiled=True
        ).astype(jnp.float32),
    )
    grad_projected = jnp.concatenate([ungroup(grad_query), key_grads, value_grads], axis=1).astype(
        jnp.bfloat16
    )
    qkv_grad = jnp.dot(normed_one.T, grad_projected, preferred_element_type=jnp.float32)
    grad_normed_one = jnp.dot(grad_projected, qkv_full.T, preferred_element_type=jnp.float32)
    grad_tokens_norm, grad_shift_one, grad_scale_one = tokens_back(grad_normed_one)
    tokens_grad = grad_residual + grad_tokens_norm
    grad_modulation = jnp.concatenate(
        [
            grad_shift_one,
            grad_scale_one,
            grad_gate_one,
            grad_shift_two,
            grad_scale_two,
            grad_gate_two,
        ]
    )
    cond_float = cond_act.astype(jnp.float32)
    rest = (
        qkv_grad,
        out_grad,
        router_grad,
        shared_in_grad,
        shared_out_grad,
        expert_in_grad,
        expert_out_grad,
    )
    grads = (cond_float[:, None] * grad_modulation[None, :],) + rest
    return (block_rows, tokens_grad, grads, cond_float, grad_modulation)


def on_device(
    tokens,
    timesteps,
    routes,
    ada_weight,
    qkv_weight,
    out_weight,
    router_weight,
    shared_in_weight,
    shared_out_weight,
    expert_in_weight,
    expert_out_weight,
    cotangent,
):
    shards = (
        ada_weight,
        qkv_weight,
        out_weight,
        router_weight,
        shared_in_weight,
        shared_out_weight,
        expert_in_weight,
        expert_out_weight,
    )
    block_list = []
    grad_list = []
    totals = None
    for micro_index in range(tokens.shape[0]):
        weights = fetch_weights(shards)
        block_rows, tokens_grad, grads, cond_float, grad_modulation = run_micro(
            weights,
            tokens[micro_index, 0],
            timesteps[micro_index, 0],
            routes[micro_index, 0],
            cotangent[micro_index, 0],
        )
        grads = reduce_grads(grads)
        totals = grads if totals is None else jax.tree.map(jnp.add, totals, grads)
        block_list.append(block_rows)
        grad_list.append(tokens_grad)
    ada_grad = totals[0]
    others = totals[1:]
    block_out = jnp.stack(block_list)[:, None]
    tokens_grads = jnp.stack(grad_list)[:, None]
    return (
        block_out,
        tokens_grads,
        ada_grad,
        others[0],
        others[1],
        others[2],
        others[3],
        others[4],
        others[5],
        others[6],
    )


def solution(mesh):
    in_specs = (
        P(None, "dp", "blk", None),
        P(None, "dp"),
        P(None, "dp", "blk", None),
        P("dp", "blk"),
        P("dp", "blk"),
        P("dp", "blk"),
        P("dp", "blk"),
        P("dp", "blk"),
        P("blk", "dp"),
        P("blk", "dp", None),
        P("blk", None, "dp"),
        P(None, "dp", "blk", None),
    )
    out_specs = (
        P(None, "dp", "blk", None),
        P(None, "dp", "blk", None),
        P("dp", "blk"),
        P("dp", "blk"),
        P("dp", "blk"),
        P("dp", "blk"),
        P("dp", "blk"),
        P("blk", "dp"),
        P("blk", "dp", None),
        P("blk", None, "dp"),
    )
    return jax.shard_map(
        on_device, mesh=mesh, in_specs=in_specs, out_specs=out_specs, check_vma=False
    )
```

profile of v0, /device:TPU:0, one launch (start us, length us, event | category | flops | bytes accessed | tf_op | source)
XLA Modules:
  0.0 2190.7 jit_solution(1355818135361958347)
XLA Ops:
  9.5 49.4 %all-gather.12.cloned.1.call-done = bf16[768,1152]{1,0:T(8,128)(2,1)} async-done(((bf16[96,1152]{1,0:T(8,128)(2,1)}), bf16[768,1152]{1,0:T(8,128)(2,1)}) %all-gather.12.cloned.1.call-update) | async-done | bytes 1769488 | tf_op jit(solution)/shard_map/all_gather | solution.py:108
  58.9 33.9 %all_gather.70 = bf16[768,576]{1,0:T(8,128)(2,1)S(1)} all-gather(bf16[96,576]{1,0:T(8,128)(2,1)} %param.26), channel_id=1, replica_groups=mesh['dp'=8,'blk'=4] {'dp'}, dimensions={0}, use_global_device_ids=true | all-gather | bytes 995328 | tf_op jit(solution)/shard_map/all_gather | solution.py:109
  94.2 31.7 %all_gather.74 = bf16[768,192]{1,0:T(8,128)(2,1)S(1)} all-gather(bf16[96,192]{1,0:T(8,128)(2,1)S(1)} %copy-done.66), channel_id=1, replica_groups=mesh['dp'=8,'blk'=4] {'dp'}, dimensions={0}, use_global_device_ids=true | all-gather | bytes 331776 | tf_op jit(solution)/shard_map/all_gather | solution.py:110
  134.2 18.5 all-reduce
  161.9 37.3 %all-gather.14.cloned.1.call-done = bf16[768,4608]{1,0:T(8,128)(2,1)} async-done(((bf16[768,1152]{1,0:T(8,128)(2,1)}), bf16[768,4608]{1,0:T(8,128)(2,1)}) %all-gather.14.cloned.1.call-update) | async-done | bytes 7077904 | tf_op jit(solution)/shard_map/all_gather | solution.py:118
  205.3 26.7 %all-gather.16.cloned.1.call-done = bf16[768,2304]{0,1:T(8,128)(2,1)} async-done(((bf16[768,576]{0,1:T(8,128)(2,1)}), bf16[768,2304]{0,1:T(8,128)(2,1)}) %all-gather.16.cloned.1.call-update) | async-done | bytes 3538960 | tf_op jit(solution)/shard_map/all_gather | solution.py:119
  235.4 8.7 all_gather.73
  244.6 11.0 all_gather.72
  301.3 73.1 %all-gather.28.cloned.1.call-done = bf16[1,768,3072]{2,1,0:T(8,128)(2,1)} async-done(((bf16[1,96,3072]{2,1,0:T(8,128)(2,1)}), bf16[1,768,3072]{2,1,0:T(8,128)(2,1)}) %all-gather.28.cloned.1.call-update) | async-done | bytes 4718608 | tf_op jit(solution)/shard_map/all_gather | solution.py:114
  374.3 5.9 fusion.98
  380.2 74.4 %all-gather.30.cloned.1.call-done = bf16[1,3072,768]{1,2,0:T(8,128)(2,1)} async-done(((bf16[1,3072,96]{1,2,0:T(8,128)(2,1)}), bf16[1,3072,768]{1,2,0:T(8,128)(2,1)}) %all-gather.30.cloned.1.call-update) | async-done | bytes 4718608 | tf_op jit(solution)/shard_map/all_gather | solution.py:115
  454.6 7.0 fusion.131
  469.3 6.5 fusion.174
  475.8 6.6 all-to-all-done.5
  487.0 14.1 all-gather.26.cloned.1.call-done
  533.8 11.3 while.54
  558.4 12.6 reduce-scatter.66.cloned.1.call-done
  572.1 25.3 %reduce-scatter.64.cloned.1.call-done = bf16[128,768]{1,0:T(8,128)(2,1)} async-done(((bf16[512,768]{1,0:T(8,128)(2,1)}), bf16[128,768]{1,0:T(8,128)(2,1)}) %reduce-scatter.64.cloned.1.call-update) | async-done | bytes 196624
  604.9 8.2 all_gather.84
  615.4 10.2 all_gather.85
  627.0 6.7 while.53
  676.0 6.8 fusion.126
  692.9 6.5 fusion.169
  741.6 16.3 while.55
  768.8 16.9 reduce-scatter.70.cloned.1.call-done
  786.8 24.8 %reduce-scatter.68.cloned.1.call-done = bf16[128,768]{1,0:T(8,128)(2,1)} async-done(((bf16[512,768]{1,0:T(8,128)(2,1)}), bf16[128,768]{1,0:T(8,128)(2,1)}) %reduce-scatter.68.cloned.1.call-update) | async-done | bytes 196624
  845.7 10.2 copy.178
  861.0 10.3 copy.176
  872.6 9.4 fusion.136
  882.3 10.3 all-reduce.4
  894.2 11.6 fusion.80
  905.9 21.0 copy.161
  929.7 25.4 %reduce-scatter.44.cloned.1.call-done = bf16[768,576]{0,1:T(8,128)(2,1)} async-done(((bf16[768,2304]{0,1:T(8,128)(2,1)}), bf16[768,576]{0,1:T(8,128)(2,1)}) %reduce-scatter.44.cloned.1.call-update) | async-done | bytes 884752 | tf_op jit(solution)/shard_map/reduce_scatter | solution.py:133
  958.6 46.9 %reduce-scatter.50.cloned.1.call-done = bf16[768,768]{1,0:T(8,128)(2,1)} async-done(((bf16[768,3072]{1,0:T(8,128)(2,1)}), bf16[768,768]{1,0:T(8,128)(2,1)}) %reduce-scatter.50.cloned.1.call-update) | async-done | bytes 1179664 | tf_op jit(solution)/shard_map/reduce_scatter | solution.py:142
  1005.5 50.4 %reduce-scatter.52.cloned.1.call-done = bf16[768,768]{1,0:T(8,128)(2,1)} async-done(((bf16[768,3072]{1,0:T(8,128)(2,1)}), bf16[768,768]{1,0:T(8,128)(2,1)}) %reduce-scatter.52.cloned.1.call-update) | async-done | bytes 1179664 | tf_op jit(solution)/shard_map/reduce_scatter | solution.py:142
  1059.4 47.0 %reduce-scatter.54.cloned.1.call-done = bf16[768,768]{1,0:T(8,128)(2,1)} async-done(((bf16[3072,768]{1,0:T(8,128)(2,1)}), bf16[768,768]{1,0:T(8,128)(2,1)}) %reduce-scatter.54.cloned.1.call-update) | async-done | bytes 1179664 | tf_op jit(solution)/shard_map/reduce_scatter | solution.py:145
  1106.4 50.6 %reduce-scatter.56.cloned.1.call-done = bf16[768,768]{1,0:T(8,128)(2,1)} async-done(((bf16[3072,768]{1,0:T(8,128)(2,1)}), bf16[768,768]{1,0:T(8,128)(2,1)}) %reduce-scatter.56.cloned.1.call-update) | async-done | bytes 1179664 | tf_op jit(solution)/shard_map/reduce_scatter | solution.py:145
  1167.4 6.5 fusion.81
  1174.0 49.2 %reduce-scatter.74.cloned.1.call-done = bf16[1152,768]{1,0:T(8,128)(2,1)} async-done(((bf16[4608,768]{1,0:T(8,128)(2,1)}), bf16[1152,768]{1,0:T(8,128)(2,1)}) %reduce-scatter.74.cloned.1.call-update) | async-done | bytes 1769488
  1226.0 63.6 %reduce-scatter.72.cloned.1.call-done = bf16[1152,768]{1,0:T(8,128)(2,1)} async-done(((bf16[4608,768]{1,0:T(8,128)(2,1)}), bf16[1152,768]{1,0:T(8,128)(2,1)}) %reduce-scatter.72.cloned.1.call-update) | async-done | bytes 1769488
  1298.9 55.3 %reduce-scatter.80.cloned.1.call-done = f32[96,1]{1,0:T(8,128)} async-done(((f32[768,1]{1,0:T(8,128)}), f32[96,1]{1,0:T(8,128)}) %reduce-scatter.80.cloned.1.call-update) | async-done | bytes 400
  1356.8 298.3 %all-reduce.7.cloned.1.call-done = f32[1,3072,768]{1,0,2:T(1,128)} async-done(((f32[1,3072,768]{1,0,2:T(1,128)}), f32[1,3072,768]{1,0,2:T(1,128)}) %all-reduce.7.cloned.1.call-update) | async-done | bytes 9437200
  1657.7 62.7 %reduce-scatter.78.cloned.1.call-done = f32[96,192]{1,0:T(8,128)} async-done(((f32[768,192]{1,0:T(8,128)}), f32[96,192]{1,0:T(8,128)}) %reduce-scatter.78.cloned.1.call-update) | async-done | bytes 73744
  1720.4 70.3 %reduce-scatter.76.cloned.1.call-done = f32[96,576]{1,0:T(8,128)} async-done(((f32[768,576]{1,0:T(8,128)}), f32[96,576]{1,0:T(8,128)}) %reduce-scatter.76.cloned.1.call-update) | async-done | bytes 221200
  1790.7 72.0 %reduce-scatter.60.cloned.1.call-done = f32[96,768]{1,0:T(8,128)} async-done(((f32[768,768]{1,0:T(8,128)}), f32[96,768]{1,0:T(8,128)}) %reduce-scatter.60.cloned.1.call-update) | async-done | bytes 294928 | tf_op jit(solution)/shard_map/reduce_scatter | solution.py:155
  1862.7 72.0 %reduce-scatter.82.cloned.1.call-done = f32[96,768]{1,0:T(8,128)} async-done(((f32[768,768]{1,0:T(8,128)}), f32[96,768]{1,0:T(8,128)}) %reduce-scatter.82.cloned.1.call-update) | async-done | bytes 294928
  1934.8 166.7 %reduce-scatter.62.cloned.1.call-done = f32[1,96,3072]{2,1,0:T(8,128)} async-done(((f32[1,768,3072]{2,1,0:T(8,128)}), f32[1,96,3072]{2,1,0:T(8,128)}) %reduce-scatter.62.cloned.1.call-update) | async-done | bytes 1179664 | tf_op jit(solution)/shard_map/reduce_scatter | solution.py:157
  2101.5 82.5 %reduce-scatter.58.cloned.1.call-done = f32[96,1152]{1,0:T(8,128)} async-done(((f32[768,1152]{1,0:T(8,128)}), f32[96,1152]{1,0:T(8,128)}) %reduce-scatter.58.cloned.1.call-update) | async-done | bytes 442384 | tf_op jit(solution)/shard_map/reduce_scatter | solution.py:151
  (605 shorter events, 366.8 us)
Async XLA Ops:
  7.2 87.0 %copy-start.66 = (bf16[96,192]{1,0:T(8,128)(2,1)S(1)}, bf16[96,192]{1,0:T(8,128)(2,1)}, u32[]{:S(2)}) copy-start(bf16[96,192]{1,0:T(8,128)(2,1)} %param.27) | copy-start | bytes 110596
  7.2 51.7 %all-gather.12.cloned.1.call-start = ((), (), s32[]{:S(2)}) async-start(), calls=%async_computation.29 | async-start | bytes 1990656 | tf_op jit(solution)/shard_map/all_gather | solution.py:108
  7.9 118.9 %all-gather.20.cloned.1.call-start = ((), (), s32[]{:S(2)}) async-start(), calls=%async_computation.33 | async-start | bytes 1327104 | tf_op jit(solution)/shard_map/all_gather | solution.py:112
  8.7 153.2 %all-gather.24.cloned.1.call-start = ((), (), s32[]{:S(2)}) async-start(), calls=%async_computation.35 | async-start | bytes 1327104 | tf_op jit(solution)/shard_map/all_gather | solution.py:113
  9.4 189.9 %all-gather.14.cloned.1.call-start = ((), (), s32[]{:S(2)}) async-start(), calls=%async_computation.30 | async-start | bytes 8847360 | tf_op jit(solution)/shard_map/all_gather | solution.py:118
  58.9 173.2 %all-gather.16.cloned.1.call-start = ((), (), s32[]{:S(2)}) async-start(), calls=%async_computation.31 | async-start | bytes 4423680 | tf_op jit(solution)/shard_map/all_gather | solution.py:119
  92.8 68.7 %copy-start.5 = (bf16[2,1,128,768]{3,2,1,0:T(8,128)(2,1)S(1)}, bf16[2,1,128,768]{3,2,1,0:T(8,128)(2,1)}, u32[]{:S(2)}) copy-start(bf16[2,1,128,768]{3,2,1,0:T(8,128)(2,1)} %param.22) | copy-start | bytes 1179652
  94.1 171.3 %all-gather.18.cloned.1.call-start = ((), (), s32[]{:S(2)}) async-start(), calls=%async_computation.32 | async-start | bytes 1474560 | tf_op jit(solution)/shard_map/all_gather | solution.py:120
  126.8 165.5 %all-gather.22.cloned.1.call-start = ((), (), s32[]{:S(2)}) async-start(), calls=%async_computation.34 | async-start | bytes 5898240 | tf_op jit(solution)/shard_map/all_gather | solution.py:122
  127.5 246.8 %all-gather.28.cloned.1.call-start = ((), (), s32[]{:S(2)}) async-start(), calls=%async_computation.37 | async-start | bytes 5308416 | tf_op jit(solution)/shard_map/all_gather | solution.py:114
  128.3 326.3 %all-gather.30.cloned.1.call-start = ((), (), s32[]{:S(2)}) async-start(), calls=%async_computation.38 | async-start | bytes 5308416 | tf_op jit(solution)/shard_map/all_gather | solution.py:115
  129.0 372.1 %all-gather.26.cloned.1.call-start = ((), (), s32[]{:S(2)}) async-start(), calls=%async_computation.36 | async-start | bytes 5898240 | tf_op jit(solution)/shard_map/all_gather | solution.py:123
  161.9 70.2 %copy-start.73 = (f32[128]{0:T(128)}, f32[128]{0:T(128)S(1)}, u32[]{:S(2)}) copy-start(f32[128]{0:T(128)S(1)} %fusion.271) | copy-start | bytes 1540
  204.3 52.7 %copy-start.64 = (f32[768]{0:T(1024)}, f32[768]{0:T(1024)S(1)}, u32[]{:S(2)}) copy-start(f32[768]{0:T(1024)S(1)} %get-tuple-element.353) | copy-start | bytes 9220
  268.9 258.6 %copy-start.17 = (f32[128,768]{1,0:T(8,128)}, f32[128,768]{1,0:T(8,128)S(1)}, u32[]{:S(2)}) copy-start(f32[128,768]{1,0:T(8,128)S(1)} %get-tuple-element.333) | copy-start | bytes 1179652
  284.8 12.2 all-to-all-start
  296.9 157.7 %all-to-all-start.4 = ((bf16[4,1,68,768]{3,2,1,0:T(8,128)(2,1)}), bf16[4,1,68,768]{3,2,1,0:T(8,128)(2,1)}, u32[]{:S(2)}, u32[]{:S(2)}) async-start(bf16[4,1,68,768]{3,2,1,0:T(8,128)(2,1)} %get-tuple-element.375), calls=%async_computation.4 | async-start | bytes 884736 | tf_op jit(solution)/shard_map/all_to_all | solution.py:237
  465.2 17.2 all-to-all-start.5
  482.4 29.8 %all-to-all-start.1 = ((bf16[4,1,68,768]{3,2,1,0:T(8,128)(2,1)}), bf16[4,1,68,768]{3,2,1,0:T(8,128)(2,1)}, u32[]{:S(2)}, u32[]{:S(2)}) async-start(bf16[4,1,68,768]{3,2,1,0:T(8,128)(2,1)} %fusion.174), calls=%async_computation.1 | async-start | bytes 884736 | tf_op jit(solution)/shard_map/all_to_all | solution.py:219
  486.5 84.5 %reduce-scatter.66.cloned.1.call-start = ((), (), s32[]{:S(2)}) async-start(), calls=%async_computation.51 | async-start | bytes 983040
  547.5 49.8 %reduce-scatter.64.cloned.1.call-start = ((), (), s32[]{:S(2)}) async-start(), calls=%async_computation.50 | async-start | bytes 983040
  651.5 12.2 all-to-all-start.2
  663.6 12.4 all-to-all-start.6
  688.7 12.2 all-to-all-start.7
  700.9 15.7 all-to-all-start.3
  705.0 80.6 %reduce-scatter.70.cloned.1.call-start = ((), (), s32[]{:S(2)}) async-start(), calls=%async_computation.53 | async-start | bytes 983040
  760.9 50.7 %reduce-scatter.68.cloned.1.call-start = ((), (), s32[]{:S(2)}) async-start(), calls=%async_computation.52 | async-start | bytes 983040
  762.1 165.1 %reduce-scatter.46.cloned.1.call-start = ((), (), s32[]{:S(2)}) async-start(), calls=%async_computation.41 | async-start | bytes 1474560 | tf_op jit(solution)/shard_map/reduce_scatter | solution.py:136
  764.0 163.2 %reduce-scatter.48.cloned.1.call-start = ((), (), s32[]{:S(2)}) async-start(), calls=%async_computation.42 | async-start | bytes 1474560 | tf_op jit(solution)/shard_map/reduce_scatter | solution.py:136
  765.7 46.9 %copy-start.57 = (bf16[3,128,4,64]{1,3,2,0:T(8,128)(2,1)S(1)}, bf16[3,128,4,64]{1,3,2,0:T(8,128)(2,1)}, u32[]{:S(2)}) copy-start(bf16[3,128,4,64]{1,3,2,0:T(8,128)(2,1)} %copy-done.56) | copy-start | bytes 589828
  765.7 164.0 %reduce-scatter.42.cloned.1.call-start = ((), (), s32[]{:S(2)}) async-start(), calls=%async_computation.39 | async-start | bytes 4423680 | tf_op jit(solution)/shard_map/reduce_scatter | solution.py:133
  768.7 186.4 %reduce-scatter.44.cloned.1.call-start = ((), (), s32[]{:S(2)}) async-start(), calls=%async_computation.40 | async-start | bytes 4423680 | tf_op jit(solution)/shard_map/reduce_scatter | solution.py:133
  815.7 189.9 %reduce-scatter.50.cloned.1.call-start = ((), (), s32[]{:S(2)}) async-start(), calls=%async_computation.43 | async-start | bytes 5898240 | tf_op jit(solution)/shard_map/reduce_scatter | solution.py:142
  819.3 236.6 %reduce-scatter.52.cloned.1.call-start = ((), (), s32[]{:S(2)}) async-start(), calls=%async_computation.44 | async-start | bytes 5898240 | tf_op jit(solution)/shard_map/reduce_scatter | solution.py:142
  824.1 282.3 %reduce-scatter.54.cloned.1.call-start = ((), (), s32[]{:S(2)}) async-start(), calls=%async_computation.45 | async-start | bytes 5898240 | tf_op jit(solution)/shard_map/reduce_scatter | solution.py:145
  829.5 327.5 %reduce-scatter.56.cloned.1.call-start = ((), (), s32[]{:S(2)}) async-start(), calls=%async_computation.46 | async-start | bytes 5898240 | tf_op jit(solution)/shard_map/reduce_scatter | solution.py:145
  834.7 388.5 %reduce-scatter.74.cloned.1.call-start = ((), (), s32[]{:S(2)}) async-start(), calls=%async_computation.55 | async-start | bytes 8847360
  856.0 433.5 %reduce-scatter.72.cloned.1.call-start = ((), (), s32[]{:S(2)}) async-start(), calls=%async_computation.54 | async-start | bytes 8847360
  871.4 482.9 %reduce-scatter.80.cloned.1.call-start = ((), (), s32[]{:S(2)}) async-start(), calls=%async_computation.58 | async-start | bytes 442368
  894.2 760.9 %all-reduce.7.cloned.1.call-start = ((), (), s32[]{:S(2)}) async-start(), calls=%async_computation.60 | async-start | bytes 18874368
  926.9 793.5 %reduce-scatter.78.cloned.1.call-start = ((), (), s32[]{:S(2)}) async-start(), calls=%async_computation.57 | async-start | bytes 884736
  929.6 861.1 %reduce-scatter.76.cloned.1.call-start = ((), (), s32[]{:S(2)}) async-start(), calls=%async_computation.56 | async-start | bytes 2211840
  958.5 904.2 %reduce-scatter.60.cloned.1.call-start = ((), (), s32[]{:S(2)}) async-start(), calls=%async_computation.48 | async-start | bytes 2654208 | tf_op jit(solution)/shard_map/reduce_scatter | solution.py:155
  1059.3 875.5 %reduce-scatter.82.cloned.1.call-start = ((), (), s32[]{:S(2)}) async-start(), calls=%async_computation.59 | async-start | bytes 2654208
  1163.5 937.9 %reduce-scatter.62.cloned.1.call-start = ((), (), s32[]{:S(2)}) async-start(), calls=%async_computation.49 | async-start | bytes 10616832 | tf_op jit(solution)/shard_map/reduce_scatter | solution.py:157
  1173.9 1010.0 %reduce-scatter.58.cloned.1.call-start = ((), (), s32[]{:S(2)}) async-start(), calls=%async_computation.47 | async-start | bytes 3981312 | tf_op jit(solution)/shard_map/reduce_scatter | solution.py:151
  1297.1 58.5 %copy-start.50 = (f32[128,768]{1,0:T(8,128)S(1)}, f32[128,768]{1,0:T(8,128)}, u32[]{:S(2)}) copy-start(f32[128,768]{1,0:T(8,128)} %copy-done.49) | copy-start | bytes 1179652
  1297.1 58.8 %copy-start.46 = (f32[1,128,768]{2,1,0:T(8,128)S(1)}, f32[1,128,768]{2,1,0:T(8,128)}, u32[]{:S(2)}) copy-start(f32[1,128,768]{2,1,0:T(8,128)} %get-tuple-element.342) | copy-start | bytes 1179652
  (95 other events, 631.3 us)
Sparse Core Ops, SparseCore 0:
  10.2 48.6 all-gather.11
  61.0 44.7 all-gather.19
  108.1 40.0 all-gather.23
  149.5 49.6 all-gather.13
  201.2 30.7 all-gather.15
  234.0 19.1 all-gather.17
  254.8 37.4 all-gather.21
  294.4 79.8 all-gather.27
  376.5 78.0 all-gather.29
  456.0 45.0 all-gather.25
  547.7 23.2 reduce-scatter.65
  574.1 23.2 reduce-scatter.63
  761.0 24.6 reduce-scatter.69
  788.2 23.2 reduce-scatter.67
  814.5 25.7 reduce-scatter.45
  843.4 25.6 reduce-scatter.47
  871.6 40.4 reduce-scatter.41
  914.6 40.4 reduce-scatter.43
  957.6 47.8 reduce-scatter.49
  1008.1 47.8 reduce-scatter.51
  1058.5 47.8 reduce-scatter.53
  1109.1 47.8 reduce-scatter.55
  1159.5 63.6 reduce-scatter.73
  1225.8 63.7 reduce-scatter.71
  1292.8 61.3 reduce-scatter.79
  1357.9 297.1 all-reduce.6
  1658.9 61.5 reduce-scatter.77
  1724.9 65.7 reduce-scatter.75
  1794.8 67.9 reduce-scatter.59
  1866.7 68.0 reduce-scatter.81
  1938.9 162.4 reduce-scatter.61
  2105.7 78.2 reduce-scatter.57
where the time goes:
time: 2200 us; the launch traced here: 2190 us
  waiting for transfers between devices  1590 us (72%)
  matrix products  188 us (9%)
  local copies, waits for them, and re-layouts  162 us (7%)
  blocking collectives  138 us (6%)
  other arithmetic  57.6 us (3%)
  starting transfers between devices  36.3 us (2%)
    unnamed x43, waiting for transfers between devices  756 us
    reduce_scatter x1, waiting for transfers between devices, reduce_grads(): lax.psum_scatter(grads[6], 'dp', scatter_dimension=1, tiled=True)  167 us
    reduce_scatter x2, waiting for transfers between devices, reduce_grads(): lax.psum_scatter(grads[5].astype(jnp.bfloat16), 'blk', scatter_dimension=...  97.6 us
    reduce_scatter x2, waiting for transfers between devices, reduce_grads(): lax.psum_scatter(grads[4].astype(jnp.bfloat16), 'blk', scatter_dimension=...  97.4 us
    reduce_scatter x1, waiting for transfers between devices, reduce_grads(): lax.psum_scatter(dense_parts[0], 'dp', scatter_dimension=0, tiled=True)  82.5 us
    all_gather x1, waiting for transfers between devices, fetch_weights(): lax.all_gather(shards[7], 'dp', axis=2, tiled=True)  74.4 us
    all_gather x1, waiting for transfers between devices, fetch_weights(): lax.all_gather(shards[6], 'dp', axis=1, tiled=True)  73.1 us
    reduce_scatter x1, waiting for transfers between devices, reduce_grads(): lax.psum_scatter(dense_parts[4], 'dp', scatter_dimension=0, tiled=True)  72 us
  transfers between devices with their start and end apart: 40, of which 31 were waited for; matrix products, arithmetic and copies ran while one was open for 12% of the time, Pallas kernels for 0%

commit v1 on v0

v1 whole, which is shorter than its diff:
```python
import functools
import math

import jax
import jax.numpy as jnp
from jax import lax
from jax.experimental import pallas as pl
from jax.experimental.pallas import tpu as pltpu
from jax.sharding import PartitionSpec as P

D = 768
HEADS = 12
HEAD_DIM = 64
TOP = 2
LANES = 128
F32 = jnp.float32
BF16 = jnp.bfloat16
NN = (((1,), (0,)), ((), ()))
NT = (((1,), (1,)), ((), ()))
TN = (((0,), (0,)), ((), ()))
EPS_NORM = 1e-06
GELU_C = math.sqrt(2.0 / math.pi)
GELU_A = 0.044715
VMEM_LIMIT = 60 * 1024 * 1024


def mm(left, right, dims=NN):
    return lax.dot_general(left, right, dims, preferred_element_type=F32)


def call(kernel, out_shape, name, **kwargs):
    return pl.pallas_call(
        kernel,
        out_shape=out_shape,
        name=name,
        compiler_params=pltpu.CompilerParams(vmem_limit_bytes=VMEM_LIMIT),
        **kwargs,
    )


def smem():
    return pl.BlockSpec(memory_space=pltpu.SMEM)


def vmem():
    return pl.BlockSpec(memory_space=pltpu.VMEM)


def shaped(shape, dtype):
    return jax.ShapeDtypeStruct(shape, dtype)


class Moves:
    def __init__(self, mesh):
        self.n_dp, self.n_blk = mesh.shape["dp"], mesh.shape["blk"]
        self.ring = 4 if self.n_dp == 8 else 0
        self.rows = D // self.n_dp if self.ring else D
        self.slots = 8 if self.ring else 1

    def info(self):
        dp, blk = lax.axis_index("dp"), lax.axis_index("blk")
        if self.ring:
            z, x = dp // 2, dp % 2
            offs = [
                (2 * ((z + self.ring - step) % self.ring) + (x ^ flip)) * self.rows
                for flip in range(2)
                for step in range(self.ring)
            ]
        else:
            offs = [jnp.zeros((), jnp.int32)]
        blocks = [blk ^ rel for rel in range(self.n_blk)]
        return jnp.stack(offs + blocks).astype(jnp.int32)

    def rotate(self, array, steps=1):
        pairs = [(d, (d + 2 * steps) % self.n_dp) for d in range(self.n_dp)]
        return lax.ppermute(array, "dp", pairs)

    def swap(self, array):
        return lax.ppermute(array, "dp", [(d, d ^ 1) for d in range(self.n_dp)])

    def flip(self, array, bit):
        return lax.ppermute(array, "blk", [(b, b ^ bit) for b in range(self.n_blk)])

    def round(self, array):
        steps = [array]
        for _ in range(self.ring - 1):
            steps.append(self.rotate(steps[-1]))
        return steps

    def whole(self, shard):
        return lax.all_gather(shard, "dp", axis=0, tiled=True)[None]

    def fold_ring(self, parts):
        travelling = parts[1].astype(BF16)
        for step in range(2, self.ring + 1):
            arrived = self.rotate(travelling).astype(F32)
            total = parts[step % self.ring] + arrived
            travelling = total.astype(BF16)
        return total

    def fold_whole(self, part):
        return lax.psum_scatter(part[0], "dp", scatter_dimension=0, tiled=True).astype(F32)


def add(left, right):
    return left.astype(F32) + right.astype(F32)


def normed(rows):
    mean = jnp.mean(rows, axis=-1, keepdims=True)
    centered = rows - mean
    var = jnp.mean(centered * centered, axis=-1, keepdims=True)
    inverse = lax.rsqrt(var + EPS_NORM)
    return centered * inverse, inverse


def norm_back(hat, inverse, grad_hat):
    mean_grad = jnp.mean(grad_hat, axis=-1, keepdims=True)
    mean_both = jnp.mean(grad_hat * hat, axis=-1, keepdims=True)
    return inverse * (grad_hat - mean_grad - hat * mean_both)


def column_sum(rows):
    return jnp.sum(rows, axis=0, keepdims=True)


def assemble_kernel(moves, widths, info, *refs):
    n_in = len(refs) - len(widths)
    ins, outs = refs[:n_in], refs[n_in:]
    n_blk, slots, rows = moves.n_blk, moves.slots, moves.rows
    per = n_blk // n_in
    for rel in range(n_blk):
        block = info[slots + rel]
        source = ins[rel // per]
        for j in range(slots):
            first = pl.multiple_of(info[j], rows)
            start = 0
            for out, width in zip(outs, widths):
                out[block, pl.ds(first, rows), :] = source[rel % per, j, :, start : start + width]
                start += width


def qkv_kernel(micro, n_blk, tokens, mod, weight, normed_out, out, wide):
    length = tokens.shape[0] // micro
    for m in range(micro):
        rows = slice(m * length, (m + 1) * length)
        hat, _ = normed(tokens[rows, :].astype(F32))
        values = hat * (1.0 + mod[m, 1:2, :]) + mod[m, 0:1, :]
        normed_out[rows, :] = values.astype(BF16)
    rows = normed_out[...]
    width = weight.shape[2]
    for b in range(n_blk):
        wide[:, b * width : (b + 1) * width] = mm(rows, weight[b]).astype(BF16)
    part = D // n_blk
    for h in range(n_blk):
        for i in range(3):
            out[h, :, i * part : (i + 1) * part] = wide[:, i * D + h * part : i * D + (h + 1) * part]


def head_rows(ref, start):
    block = ref[:, :, start : start + HEAD_DIM]
    return block.reshape(block.shape[0] * block.shape[1], HEAD_DIM)


def softmax_rows(query, key):
    scores = mm(query, key, NT) * (1.0 / math.sqrt(HEAD_DIM))
    raised = jnp.exp(scores - jnp.max(scores, axis=-1, keepdims=True))
    return raised / jnp.sum(raised, axis=-1, keepdims=True)


def attend_kernel(projected, out):
    part = out.shape[2]
    sources, length = out.shape[0], out.shape[1]
    for start in range(0, part, HEAD_DIM):
        query, key, value = (head_rows(projected, i * part + start) for i in range(3))
        probs = softmax_rows(query, key).astype(BF16)
        mixed = mm(probs, value).astype(BF16)
        out[:, :, start : start + HEAD_DIM] = mixed.reshape(sources, length, HEAD_DIM)


def attend_back_kernel(projected, grad_mixed, out):
    part = grad_mixed.shape[2]
    sources, length = out.shape[0], out.shape[1]
    scale = 1.0 / math.sqrt(HEAD_DIM)
    for start in range(0, part, HEAD_DIM):
        query, key, value = (head_rows(projected, i * part + start) for i in range(3))
        grad = head_rows(grad_mixed, start)
        probs = softmax_rows(query, key)
        grad_probs = mm(grad, value, NT)
        inner = jnp.sum(probs * grad_probs, axis=-1, keepdims=True)
        grad_scores = (probs * (grad_probs - inner)).astype(BF16)
        grads = (
            mm(grad_scores, key) * scale,
            mm(grad_scores, query, TN) * scale,
            mm(probs.astype(BF16), grad, TN),
        )
        for i, part_grad in enumerate(grads):
            out[:, :, i * part + start : i * part + start + HEAD_DIM] = part_grad.astype(
                BF16
            ).reshape(sources, length, HEAD_DIM)


def pick(routes, k, count):
    lanes = lax.broadcasted_iota(jnp.int32, (routes.shape[0], count), 1)
    return lanes == routes[:, k : k + 1]


def residual_kernel(
    micro, n_blk, mixed_in, tokens, mod, out_weight, router, cotangent, routes, slots_t,
    mixed, attended, residual, normed_two, grad_shared, probs, send,
):
    part = D // n_blk
    for h in range(n_blk):
        mixed[:, h * part : (h + 1) * part] = mixed_in[h]
    all_mixed = mixed[...]
    for b in range(n_blk):
        attended[:, b * part : (b + 1) * part] = mm(all_mixed, out_weight[b])
    length = tokens.shape[0] // micro
    for m in range(micro):
        rows = slice(m * length, (m + 1) * length)
        stream = tokens[rows, :].astype(F32) + mod[m, 2:3, :] * attended[rows, :]
        residual[rows, :] = stream
        hat, _ = normed(stream)
        normed_two[rows, :] = (hat * (1.0 + mod[m, 4:5, :]) + mod[m, 3:4, :]).astype(BF16)
    rows_two = normed_two[...]
    logits = mm(rows_two, router[...], NT)
    chosen = [
        jnp.sum(jnp.where(pick(routes, k, LANES), logits, 0.0), axis=-1, keepdims=True)
        for k in range(TOP)
    ]
    top = functools.reduce(jnp.maximum, chosen)
    raised = [jnp.exp(value - top) for value in chosen]
    total = functools.reduce(jnp.add, raised)
    gates = [value / total for value in raised]
    for k in range(TOP):
        probs[:, k : k + 1] = gates[k]
    grad_mix = jnp.concatenate(
        [
            cotangent[m * length : (m + 1) * length, :].astype(F32) * mod[m, 5:6, :]
            for m in range(micro)
        ]
    )
    grad_shared[...] = grad_mix.astype(BF16)
    experts, _, room, _ = send.shape
    index = lax.broadcasted_iota(jnp.int32, (experts * room, micro * length), 0)
    holds = [(index == slots_t[k : k + 1, :]).astype(BF16) for k in range(TOP)]
    sent = mm(functools.reduce(jnp.add, holds), rows_two).astype(BF16)
    send[:, 0] = sent.reshape(experts, room, D)
    pairs = [(gates[k] * grad_mix).astype(BF16) for k in range(TOP)]
    sent = functools.reduce(jnp.add, [mm(holds[k], pairs[k]) for k in range(TOP)]).astype(BF16)
    send[:, 1] = sent.reshape(experts, room, D)


def expert_kernel(moves, maps, first, last, tile, info, rows_ref, grads_ref, *refs):
    refs = list(refs)
    acc = [] if first else [refs.pop(0), refs.pop(0)]
    weights = [refs.pop(0) for _ in maps]
    if last:
        both = refs.pop(0)
    else:
        totals = [refs.pop(0), refs.pop(0)]
    outs = [refs.pop(0) for _ in maps]
    w_in, w_out, g_in, g_out = refs[:4]
    if last:
        totals = refs[4:6]
    step = pl.program_id(0)
    rows = rows_ref[...].reshape(-1, D)
    grads = grads_ref[...].reshape(-1, D)

    @pl.when(step == 0)
    def _():
        for i in range(2):
            totals[i][...] = jnp.zeros_like(totals[i]) if first else acc[i][...]

    for ref, slots in zip(weights, maps):
        for k, j in enumerate(slots):
            at = pl.ds(pl.multiple_of(info[j], moves.rows), moves.rows)
            w_in[at, :] = ref[k, :, :tile]
            w_out[at, :] = ref[k, :, tile:]
    pre = mm(rows, w_in[...])
    squared = pre * pre
    bend = jnp.tanh(GELU_C * pre * (1.0 + GELU_A * squared))
    half = 0.5 * (1.0 + bend)
    act = (pre * half).astype(BF16)
    slope = half + 0.5 * pre * (1.0 - bend * bend) * (GELU_C * (1.0 + 3.0 * GELU_A * squared))
    totals[0][...] += mm(act, w_out[...], NT)
    grad_pre = (mm(grads, w_out[...]) * slope).astype(BF16)
    totals[1][...] += mm(grad_pre, w_in[...], NT)
    g_in[...] = mm(rows, grad_pre, TN).astype(BF16)
    g_out[...] = mm(grads, act, TN).astype(BF16)
    for ref, slots in zip(outs, maps):
        for k, j in enumerate(slots):
            at = pl.ds(pl.multiple_of(info[j], moves.rows), moves.rows)
            ref[k, :, :tile] = g_in[at, :]
            ref[k, :, tile:] = g_out[at, :]
    if last:

        @pl.when(step == pl.num_programs(0) - 1)
        def _():
            for i in range(2):
                both[:, i] = totals[i][...].astype(BF16).reshape(both.shape[0], *both.shape[2:])


def expert_part(moves, info, rows, grads, acc, weights, maps, tile, out_both, name):
    first, last = acc is None, out_both is not None
    steps = weights[0].shape[2] // (2 * tile)
    count = math.prod(rows[0].shape[i] for i in rows[2])
    kernel = functools.partial(expert_kernel, moves, maps, first, last, tile)
    w_specs = [
        pl.BlockSpec((w.shape[0], w.shape[1], 2 * tile), lambda j: (0, 0, j)) for w in weights
    ]
    in_specs = [smem(), rows[1], grads[1]]
    operands = [info, rows[0], grads[0]]
    flat = pl.BlockSpec((count, D), lambda j: (0, 0))
    if not first:
        in_specs += [flat, flat]
        operands += list(acc)
    out_specs, out_shape = [], []
    scratch = [pltpu.VMEM((D, tile), BF16) for _ in range(4)]
    if last:
        out_specs.append(pl.BlockSpec(out_both, lambda j: (0,) * len(out_both)))
        out_shape.append(shaped(out_both, BF16))
        scratch += [pltpu.VMEM((count, D), F32) for _ in range(2)]
    else:
        out_specs += [flat, flat]
        out_shape += [shaped((count, D), F32)] * 2
    results = call(
        kernel,
        out_shape + [shaped(w.shape, BF16) for w in weights],
        name,
        grid=(steps,),
        in_specs=in_specs + w_specs,
        out_specs=out_specs + w_specs,
        scratch_shapes=scratch,
        cost_estimate=pl.CostEstimate(
            flops=12 * count * D * tile * steps,
            bytes_accessed=16 * D * tile * steps,
            transcendentals=count * tile * steps,
        ),
    )(*operands, *weights)
    if last:
        return results[0], results[1:]
    return results[:2], results[2:]


def middle_kernel(
    micro, n_blk, moves, info, back, routes, slots, probs, shared_val, shared_grad, residual, attended, mixed, normed_two,
    mod, out_weight, router, cotangent,
    block_out, grad_residual, grad_mod, grad_router, out_keep, out_send, grad_mixed, grad_attended, scratch,
):
    part = D // n_blk
    length = residual.shape[0] // micro
    experts, _, room, _ = back.shape
    values = back[:, 0].reshape(experts * room, D)
    grads = back[:, 1].reshape(experts * room, D)
    index = lax.broadcasted_iota(jnp.int32, (micro * length, experts * room), 1)
    holds = [(index == slots[:, k : k + 1]).astype(BF16) for k in range(TOP)]
    routed = [mm(holds[k], values) for k in range(TOP)]
    gates = [probs[:, k : k + 1] for k in range(TOP)]
    mixture = shared_val[...] + functools.reduce(
        jnp.add, [gates[k] * routed[k] for k in range(TOP)]
    )
    given = cotangent[...].astype(F32)
    grad_gates = []
    grad_mix = []
    for m in range(micro):
        rows = slice(m * length, (m + 1) * length)
        gate = mod[m, 5:6, :]
        block_out[rows, :] = (residual[rows, :] + gate * mixture[rows]).astype(BF16)
        grad_mod[m, 3:4, :] = column_sum(given[rows] * mixture[rows])
        grad_mix.append(given[rows] * gate)
    grad_mix = jnp.concatenate(grad_mix)
    grad_gates = [jnp.sum(grad_mix * routed[k], axis=-1, keepdims=True) for k in range(TOP)]
    inner = functools.reduce(jnp.add, [gates[k] * grad_gates[k] for k in range(TOP)])
    grad_logits = functools.reduce(
        jnp.add,
        [
            jnp.where(pick(routes, k, LANES), gates[k] * (grad_gates[k] - inner), 0.0)
            for k in range(TOP)
        ],
    ).astype(BF16)
    grad_router[...] = mm(grad_logits, normed_two[...], TN)
    grad_two = (
        shared_grad[...]
        + mm(functools.reduce(jnp.add, holds), grads)
        + mm(grad_logits, router[...])
    )
    for m in range(micro):
        rows = slice(m * length, (m + 1) * length)
        hat, inverse = normed(residual[rows, :])
        own = grad_two[rows]
        grad_mod[m, 1:2, :] = column_sum(own)
        grad_mod[m, 2:3, :] = column_sum(own * hat)
        total = given[rows] + norm_back(hat, inverse, own * (1.0 + mod[m, 4:5, :]))
        grad_residual[rows, :] = total
        grad_mod[m, 0:1, :] = column_sum(total * attended[rows, :])
        grad_attended[rows, :] = (total * mod[m, 2:3, :]).astype(BF16)
    all_mixed = mixed[...]
    back_mixed = functools.reduce(
        jnp.add,
        [
            mm(grad_attended[:, b * part : (b + 1) * part], out_weight[b], NT)
            for b in range(n_blk)
        ],
    ).astype(BF16)
    for h in range(n_blk):
        grad_mixed[h] = back_mixed[:, h * part : (h + 1) * part]
    for b in range(n_blk):
        scratch[b] = mm(all_mixed, grad_attended[:, b * part : (b + 1) * part], TN).astype(BF16)
    emit(moves, info, n_blk, lambda block: scratch.at[block], out_keep, out_send)


def emit(moves, info, n_blk, source, keep, send):
    for rel in range(n_blk):
        target = send if rel % 2 else keep
        held = source(info[moves.slots + rel])
        for j in range(moves.slots):
            first = pl.multiple_of(info[j], moves.rows)
            target[rel // 2, j] = held[pl.ds(first, moves.rows), :]


def qkv_grad_kernel(n_blk, moves, info, arrived, normed_one, keep, send, wide, blocks, held):
    part = D // n_blk
    for h in range(n_blk):
        for i in range(3):
            wide[:, i * D + h * part : i * D + (h + 1) * part] = arrived[h, :, i * part : (i + 1) * part]
    width = blocks.shape[2]
    for b in range(n_blk):
        blocks[b] = wide[:, b * width : (b + 1) * width]
    rows = normed_one[...]

    def source(block):
        held[...] = mm(rows, blocks[block], TN).astype(BF16)
        return held

    emit(moves, info, n_blk, source, keep, send)


def tokens_grad_kernel(micro, n_blk, blocks, weight, tokens, mod, grad_residual, out, grad_mod):
    width = blocks.shape[2]
    grad_one = functools.reduce(
        jnp.add, [mm(blocks[b], weight[b], NT) for b in range(n_blk)]
    )
    length = tokens.shape[0] // micro
    for m in range(micro):
        rows = slice(m * length, (m + 1) * length)
        hat, inverse = normed(tokens[rows, :].astype(F32))
        own = grad_one[rows]
        grad_mod[m, 0:1, :] = column_sum(own)
        grad_mod[m, 1:2, :] = column_sum(own * hat)
        out[rows, :] = grad_residual[rows, :] + norm_back(hat, inverse, own * (1.0 + mod[m, 1:2, :]))


def by_tile(left, right, tile):
    rows, columns = left.shape
    pair = jnp.stack([left.reshape(rows, -1, tile), right.reshape(rows, -1, tile)], axis=2)
    return pair.reshape(rows, 2 * columns)


def from_tiles(packed, tile):
    rows, columns = packed.shape
    pair = packed.reshape(rows, -1, 2, tile)
    return pair[:, :, 0].reshape(rows, -1), pair[:, :, 1].reshape(rows, -1)


def slots_of(routes, experts, room):
    count = routes.shape[0]
    hot = routes[:, :, None] == jnp.arange(experts, dtype=jnp.int32)
    named = jnp.sum(hot.astype(BF16), axis=1)
    before = jnp.arange(count)[:, None] > jnp.arange(count)[None, :]
    rank = mm(before.astype(BF16), named)
    ranks = jnp.sum(jnp.where(hot, rank[:, None, :], 0.0), axis=2).astype(jnp.int32)
    return routes * room + ranks


def on_device(moves, tokens, timesteps, routes, ada, qkv, out_w, router, shared_in, shared_out, expert_in, expert_out, cotangent):
    micro, _, length, _ = tokens.shape
    count = micro * length
    n_dp, n_blk = moves.n_dp, moves.n_blk
    experts = n_blk
    capacity = length * TOP // experts + max(2, length // 32)
    room = -(-micro * capacity // 16) * 16
    shard = D // n_dp
    info = moves.info()
    dp_at = lax.axis_index("dp")

    tokens_2d = tokens.reshape(count, D)
    given = cotangent.reshape(count, D)
    routes_2d = routes.reshape(count, TOP)

    pack_a = jnp.concatenate([qkv, out_w], axis=1)
    tile = shared_in.shape[1]
    pack_b = by_tile(shared_in, shared_out.T, tile)
    ff = expert_in.shape[2]
    chunk = ff // 4
    e_out = expert_out[0].T
    packs_e = [
        by_tile(expert_in[0][:, c : c + chunk], e_out[:, c : c + chunk], tile)
        for c in range(0, ff, chunk)
    ]

    steps_all = lax.all_gather(timesteps[:, 0], "dp", axis=0)
    half = D // 2
    column = dp_at * shard + jnp.arange(shard)
    frequency = jnp.exp(-math.log(10000.0) * (column % half).astype(F32) / half)
    angles = steps_all[:, :, None].astype(F32) * frequency
    cond = jnp.where(column < half, jnp.cos(angles), jnp.sin(angles))
    cond = jax.nn.silu(cond).astype(BF16)
    partial_mod = jnp.einsum("dmr,rc->dmc", cond, ada, preferred_element_type=F32)
    wide = ada.shape[1]
    payload = jnp.concatenate(
        [
            partial_mod.reshape(n_dp, micro * wide),
            jnp.broadcast_to(router[:, 0].astype(F32)[None], (n_dp, shard)),
        ],
        axis=1,
    )
    payload = jnp.broadcast_to(payload[:, None], (n_dp, n_blk, payload.shape[1]))
    payload = payload.reshape(n_dp * n_blk, -1)
    arrived = lax.all_to_all(payload, ("dp", "blk"), 0, 0, tiled=True).reshape(n_dp, n_blk, -1)
    mod = jnp.sum(arrived[:, :, : micro * wide], axis=0).reshape(n_blk, micro, wide)
    mod = mod.transpose(1, 0, 2).reshape(micro, 6, D)
    router_t = arrived[:, :, micro * wide :].transpose(1, 0, 2).reshape(n_blk, D).astype(BF16)
    router_t = jnp.pad(router_t, ((0, LANES - n_blk), (0, 0)))

    if moves.ring:
        held = jnp.stack([moves.rotate(pack_a, s) if s else pack_a for s in range(moves.ring)])
        held = jnp.concatenate([held, moves.swap(held)])
    else:
        held = moves.whole(pack_a)
    held = held[None]
    bit = 2
    while bit < n_blk:
        held = jnp.concatenate([held, moves.flip(held, bit)])
        bit *= 2
    width_q, width_o = qkv.shape[1], out_w.shape[1]
    held = [held, moves.flip(held, 1)]
    order = [0, 2, 1, 3]
    blocks_info = jnp.concatenate(
        [info[: moves.slots], info[moves.slots :][jnp.array(order)]]
    )
    qkv_w, out_full = call(
        functools.partial(assemble_kernel, moves, (width_q, width_o)),
        [shaped((n_blk, D, width_q), BF16), shaped((n_blk, D, width_o), BF16)],
        "assemble",
        in_specs=[smem(), vmem(), vmem()],
    )(blocks_info, *held)

    if moves.ring:
        weights_e = []
        for pack in packs_e:
            own = moves.round(pack[None])
            weights_e.append(own + [moves.swap(a) for a in own])
        maps_e = [[j] for j in range(moves.slots)]
        both = jnp.stack([pack_b, moves.swap(pack_b)])
        own_b = moves.round(both)
        maps_b = [[s, moves.ring + s] for s in range(moves.ring)]
    else:
        weights_e = [[moves.whole(pack)] for pack in packs_e]
        maps_e = [[0]]
        own_b = [moves.whole(pack_b)]
        maps_b = [[0]]
    far_b = [moves.flip(a, 2) for a in own_b]
    weights_b = [own_b, [moves.flip(a, 1) for a in own_b], far_b, [moves.flip(a, 1) for a in far_b]]

    normed_one, projected = call(
        functools.partial(qkv_kernel, micro, n_blk),
        [shaped((count, D), BF16), shaped((n_blk, count, 3 * D // n_blk), BF16)],
        "qkv",
        scratch_shapes=[pltpu.VMEM((count, 3 * D), BF16)],
    )(tokens_2d, mod, qkv_w)
    projected = lax.all_to_all(projected, "blk", 0, 0, tiled=True)
    part = D // n_blk

    def by_micro(columns):
        return pl.BlockSpec((n_blk, length, columns), lambda m: (0, m, 0))

    mixed_out = call(
        attend_kernel,
        shaped((n_blk, count, part), BF16),
        "attend",
        grid=(micro,),
        in_specs=[by_micro(3 * part)],
        out_specs=by_micro(part),
    )(projected)
    mixed_in = lax.all_to_all(mixed_out, "blk", 0, 0, tiled=True)

    slots = slots_of(routes_2d, experts, room)
    mixed, attended, residual, normed_two, grad_shared, probs, send = call(
        functools.partial(residual_kernel, micro, n_blk),
        [
            shaped((count, D), BF16),
            shaped((count, D), F32),
            shaped((count, D), F32),
            shaped((count, D), BF16),
            shaped((count, D), BF16),
            shaped((count, TOP), F32),
            shaped((experts, 2, room, D), BF16),
        ],
        "residual",
    )(mixed_in, tokens_2d, mod, out_full, router_t, given, routes_2d, slots.T)

    to_expert = lax.all_to_all(send, "blk", 0, 0, tiled=True)
    plain = pl.BlockSpec((count, D), lambda j: (0, 0))
    acc, grads_b = None, []
    for rel in range(n_blk):
        acc, got = expert_part(
            moves, info, (normed_two, plain, (0,)), (grad_shared, plain, (0,)), acc, weights_b[rel], maps_b, tile, None, "shared"
        )
        grads_b.append(got)
    shared_val, shared_grad = acc
    specs = [pl.BlockSpec((experts, None, room, D), lambda j, i=i: (0, i, 0, 0)) for i in range(2)]
    acc, grads_e = None, []
    for c, weights in enumerate(weights_e):
        last = c == len(weights_e) - 1
        acc, got = expert_part(
            moves, info, (to_expert, specs[0], (0, 2)), (to_expert, specs[1], (0, 2)), acc, weights, maps_e, tile,
            to_expert.shape if last else None, "routed",
        )
        grads_e.append(got)
    back = lax.all_to_all(acc, "blk", 0, 0, tiled=True)

    near, far = [], []
    for rel, into in ((0, near), (2, far)):
        other = [moves.flip(a, 1) for a in grads_b[rel + 1]]
        into.extend(add(a, b) for a, b in zip(grads_b[rel], other))
    sums_b = [add(a, moves.flip(b.astype(BF16), 2)) for a, b in zip(near, far)]
    if moves.ring:
        total = moves.fold_ring(sums_b)
        own_b_grad = add(total[0], moves.swap(total[1].astype(BF16)))
    else:
        own_b_grad = moves.fold_whole(sums_b[0].astype(BF16))
    shared_in_grad, shared_out_t = from_tiles(own_b_grad, tile)

    totals_e = []
    for got in grads_e:
        if moves.ring:
            ring = moves.ring
            parts = [None] * ring
            for s in (1, 2, 3, 0):
                parts[s] = add(got[s], moves.swap(got[ring + s]))
            totals_e.append(moves.fold_ring(parts)[0])
        else:
            totals_e.append(moves.fold_whole(got[0]))
    split_e = [from_tiles(total, tile) for total in totals_e]
    expert_in_grad = jnp.concatenate([pair[0] for pair in split_e], axis=1)
    expert_out_t = jnp.concatenate([pair[1] for pair in split_e], axis=1)

    slot_rows = (n_blk // 2, moves.slots, moves.rows)
    block_out, grad_residual, grad_mod_two, grad_router, out_keep, out_send, grad_mixed = call(
        functools.partial(middle_kernel, micro, n_blk, moves),
        [
            shaped((count, D), BF16),
            shaped((count, D), F32),
            shaped((micro, 4, D), F32),
            shaped((LANES, D), F32),
            shaped(slot_rows + (width_o,), BF16),
            shaped(slot_rows + (width_o,), BF16),
            shaped((n_blk, count, part), BF16),
        ],
        "middle",
        in_specs=[smem()] + [vmem()] * 14,
        scratch_shapes=[pltpu.VMEM((count, D), BF16), pltpu.VMEM((n_blk, D, width_o), BF16)],
    )(
        info, back, routes_2d, slots, probs, shared_val, shared_grad, residual, attended, mixed, normed_two,
        mod, out_full, router_t, given,
    )

    def fold_blocks(keep, send_part):
        total = add(keep, moves.flip(send_part, 1))
        total = add(total[0], moves.flip(total[1].astype(BF16), 2))
        if not moves.ring:
            return moves.fold_whole(total.astype(BF16))
        ring = moves.ring
        total = add(total[:ring], moves.swap(total[ring:].astype(BF16)))
        return moves.fold_ring([total[s] for s in range(ring)])

    out_grad = fold_blocks(out_keep, out_send)

    grad_mixed = lax.all_to_all(grad_mixed, "blk", 0, 0, tiled=True)
    grad_projected = call(
        attend_back_kernel,
        shaped((n_blk, count, 3 * part), BF16),
        "attend_back",
        grid=(micro,),
        in_specs=[by_micro(3 * part), by_micro(part)],
        out_specs=by_micro(3 * part),
    )(projected, grad_mixed)
    arrived = lax.all_to_all(grad_projected, "blk", 0, 0, tiled=True)
    qkv_keep, qkv_send, blocks = qkv_grads(moves, info, arrived, normed_one, slot_rows, width_q)
    qkv_grad = fold_blocks(qkv_keep, qkv_send)
    tokens_grad, grad_mod_one = call(
        functools.partial(tokens_grad_kernel, micro, n_blk),
        [shaped((count, D), F32), shaped((micro, 2, D), F32)],
        "tokens_grad",
    )(blocks, qkv_w, tokens_2d, mod, grad_residual)

    grad_mod = jnp.concatenate([grad_mod_one, grad_mod_two], axis=1).reshape(micro, n_blk, wide)
    payload = jnp.concatenate(
        [
            jnp.broadcast_to(
                grad_mod.transpose(1, 0, 2).reshape(1, n_blk, micro * wide), (n_dp, n_blk, micro * wide)
            ),
            grad_router[:n_blk].reshape(n_blk, n_dp, shard).transpose(1, 0, 2),
        ],
        axis=2,
    ).reshape(n_dp * n_blk, -1)
    arrived = lax.all_to_all(payload, ("dp", "blk"), 0, 0, tiled=True).reshape(n_dp, n_blk, -1)
    item_mod = jnp.sum(arrived[:, :, : micro * wide], axis=1).reshape(n_dp * micro, wide)
    ada_grad = jnp.dot(
        cond.reshape(n_dp * micro, shard).astype(F32).T, item_mod, precision=lax.Precision.HIGHEST
    )
    router_grad = jnp.sum(arrived[:, :, micro * wide :], axis=(0, 1))[:, None]

    return (
        block_out.reshape(tokens.shape),
        tokens_grad.reshape(tokens.shape),
        ada_grad,
        qkv_grad,
        out_grad,
        router_grad,
        shared_in_grad,
        shared_out_t.T,
        expert_in_grad[None],
        expert_out_t.T[None],
    )


def qkv_grads(moves, info, arrived, normed_one, slot_rows, width):
    n_blk, count = arrived.shape[:2]

    def kernel(info, arrived, normed_one, keep, send, blocks, wide, held):
        qkv_grad_kernel(n_blk, moves, info, arrived, normed_one, keep, send, wide, blocks, held)

    return call(
        kernel,
        [
            shaped(slot_rows + (width,), BF16),
            shaped(slot_rows + (width,), BF16),
            shaped((n_blk, count, width), BF16),
        ],
        "qkv_grad",
        in_specs=[smem(), vmem(), vmem()],
        scratch_shapes=[pltpu.VMEM((count, 3 * D), BF16), pltpu.VMEM((D, width), BF16)],
    )(info, arrived, normed_one)


def solution(mesh):
    moves = Moves(mesh)
    in_specs = (
        P(None, "dp", "blk", None),
        P(None, "dp"),
        P(None, "dp", "blk", None),
        P("dp", "blk"),
        P("dp", "blk"),
        P("dp", "blk"),
        P("dp", "blk"),
        P("dp", "blk"),
        P("blk", "dp"),
        P("blk", "dp", None),
        P("blk", None, "dp"),
        P(None, "dp", "blk", None),
    )
    out_specs = (
        P(None, "dp", "blk", None),
        P(None, "dp", "blk", None),
        P("dp", "blk"),
        P("dp", "blk"),
        P("dp", "blk"),
        P("dp", "blk"),
        P("dp", "blk"),
        P("blk", "dp"),
        P("blk", "dp", None),
        P("blk", None, "dp"),
    )
    return jax.shard_map(
        functools.partial(on_device, moves),
        mesh=mesh,
        in_specs=in_specs,
        out_specs=out_specs,
        check_vma=False,
    )
```

time: 2200 us -> 703 us (0.32)
  waiting for transfers between devices: 1590 us -> 371 us
  matrix products: 188 us -> 1.67 us
  blocking collectives: 138 us -> 11 us
  Pallas kernels: 0 us -> 117 us
  local copies, waits for them, and re-layouts: 162 us -> 46.9 us
  starting transfers between devices: 36.3 us -> 101 us
    unnamed x43 -> x0, waiting for transfers between devices: 756 us -> none
    reduce_scatter x11 -> x0, waiting for transfers between devices: 542 us -> none  [the longest x1 167 us: reduce_grads(): lax.psum_scatter(grads[6], 'dp', scatter_dimension=1, tiled=True)]
    ppermute x0 -> x106, waiting for transfers between devices: none -> 326 us  [the longest x39 150 us: rotate(): return lax.ppermute(array, 'dp', pairs)]
    all_gather x10 -> x0, waiting for transfers between devices: 278 us -> none  [the longest x1 74.4 us: fetch_weights(): lax.all_gather(shards[7], 'dp', axis=2, tiled=True)]
    dot_general x86 -> x3, matrix products: 188 us -> 1.67 us  [the longest x1 1.26 us: on_device(): jnp.dot(cond.reshape(n_dp * micro, shard).astype(F32).T, item_mod, precis...]
    pallas_call x0 -> x16, Pallas kernels: none -> 117 us  [the longest x8 65.7 us: expert_part(): call(kernel, out_shape + [shaped(w.shape, BF16) for w in weights], name,...]
    all_gather x7 -> x0, blocking collectives: 109 us -> none  [the longest x1 33.9 us: fetch_weights(): lax.all_gather(shards[1], 'dp', axis=0, tiled=True)]
    ppermute x0 -> x106, starting transfers between devices: none -> 67.8 us  [the longest x37 39 us: swap(): return lax.ppermute(array, 'dp', [(d, d ^ 1) for d in range(self.n_dp)])]
  transfers between devices with their start and end apart: 40 -> 114, of which waited for: 31 -> 59; matrix products, arithmetic and copies ran while one was open for 12% -> 11% of each run, Pallas kernels for 0% -> 16%
where the time goes in v1:
time: 703 us; the launch traced here: 694 us
  waiting for transfers between devices  371 us (53%)
  Pallas kernels  117 us (17%)
  starting transfers between devices  101 us (14%)
  local copies, waits for them, and re-layouts  46.9 us (7%)
  other arithmetic  41.7 us (6%)
  blocking collectives  11 us (2%)
    ppermute x39, waiting for transfers between devices, rotate(): return lax.ppermute(array, 'dp', pairs)  150 us
    ppermute x37, waiting for transfers between devices, swap(): return lax.ppermute(array, 'dp', [(d, d ^ 1) for d in range(self.n_dp)])  120 us
    pallas_call x8, Pallas kernels, expert_part(): call(kernel, out_shape + [shaped(w.shape, BF16) for w in weights], name,...  65.7 us
    ppermute x30, waiting for transfers between devices, flip(): return lax.ppermute(array, 'blk', [(b, b ^ bit) for b in range(self.n_blk)])  55.9 us
    ppermute x37, starting transfers between devices, swap(): return lax.ppermute(array, 'dp', [(d, d ^ 1) for d in range(self.n_dp)])  39 us
    ppermute x30, starting transfers between devices, flip(): return lax.ppermute(array, 'blk', [(b, b ^ bit) for b in range(self.n_blk)])  16.7 us
    all_to_all x2, waiting for transfers between devices, on_device(): lax.all_to_all(payload, ('dp', 'blk'), 0, 0, tiled=True)  16.6 us
  transfers between devices with their start and end apart: 114, of which 59 were waited for; matrix products, arithmetic and copies ran while one was open for 11% of the time, Pallas kernels for 16%

profile of v1, /device:TPU:0, one launch (start us, length us, event | category | flops | bytes accessed | tf_op | source)
XLA Modules:
  0.0 694.0 jit_solution(8119126370223421905)
XLA Ops:
  11.6 5.5 collective-permute-done.1
  18.8 13.6 %collective-permute-done.3 = bf16[4,96,768]{2,1,0:T(8,128)(2,1)S(1)} collective-permute-done((bf16[4,96,768]{2,1,0:T(8,128)(2,1)S(1)}, bf16[4,96,768]{2,1,0:T(8,128)(2,1)S(1)}, u32[]{:S(2)}, u32[]{:S(2)}) %collective-permute-start.3) | collective-permute-done | bytes 589856 | tf_op jit(solution)/shard_map/ppermute | solution.py:79
  37.3 22.3 %collective-permute-done.4 = bf16[1,8,96,768]{3,2,1,0:T(8,128)(2,1)} collective-permute-done((bf16[1,8,96,768]{3,2,1,0:T(8,128)(2,1)S(1)}, bf16[1,8,96,768]{3,2,1,0:T(8,128)(2,1)}, u32[]{:S(2)}, u32[]{:S(2)}) %collective-permute-start.4) | collective-permute-done | bytes 1179680 | tf_op jit(solution)/shard_map/ppermute | solution.py:82
  61.7 11.0 %all-reduce.1 = s32[16]{0:T(128)S(1)} all-reduce(s32[16]{0:T(128)S(1)} %bitcast_dynamic-update-slice_fusion), channel_id=2, replica_groups=mesh['dp'=8,'blk'=4] {'dp'}, use_global_device_ids=true, to_apply=%add.1 | all-reduce | flops 16 | bytes 128
  76.5 13.6 %collective-permute-done.35.refs_1_ = bf16[2,96,1536]{2,1,0:T(8,128)(2,1)} collective-permute-done((bf16[2,96,1536]{2,1,0:T(8,128)(2,1)}, bf16[2,96,1536]{2,1,0:T(8,128)(2,1)}, u32[]{:S(2)}, u32[]{:S(2)}) %collective-permute-start.35) | collective-permute-done | bytes 589856 | tf_op jit(solution)/shard_map/ppermute | solution.py:76
  91.3 6.1 all-to-all-start
  99.4 7.2 %collective-permute-done.36.refs_2_ = bf16[2,96,1536]{2,1,0:T(8,128)(2,1)} collective-permute-done((bf16[2,96,1536]{2,1,0:T(8,128)(2,1)}, bf16[2,96,1536]{2,1,0:T(8,128)(2,1)}, u32[]{:S(2)}, u32[]{:S(2)}) %collective-permute-start.36) | collective-permute-done | bytes 589856 | tf_op jit(solution)/shard_map/ppermute | solution.py:76
  107.9 16.6 %all-to-all-done = f32[32,1,2400]{2,1,0:T(1,128)S(1)} async-done(((f32[32,1,2400]{2,1,0:T(1,128)}), f32[32,1,2400]{2,1,0:T(1,128)S(1)}, u32[]{:S(2)}, u32[]{:S(2)}) %all-to-all-start) | async-done | bytes 307232 | tf_op jit(solution)/shard_map/all_to_all | solution.py:520
  126.1 5.5 assemble.1
  147.9 11.4 %all-to-all-done.1 = bf16[4,256,576]{1,2,0:T(8,128)(2,1)S(1)} async-done(((bf16[4,256,576]{1,2,0:T(8,128)(2,1)}), bf16[4,256,576]{1,2,0:T(8,128)(2,1)S(1)}, u32[]{:S(2)}, u32[]{:S(2)}) %all-to-all-start.1) | async-done | bytes 1179680 | tf_op jit(solution)/shard_map/all_to_all | solution.py:572
  160.8 6.2 attend.1
  175.1 9.5 %collective-permute-done.44.refs_4_ = bf16[2,96,1536]{2,1,0:T(8,128)(2,1)S(1)} collective-permute-done((bf16[2,96,1536]{2,1,0:T(8,128)(2,1)}, bf16[2,96,1536]{2,1,0:T(8,128)(2,1)S(1)}, u32[]{:S(2)}, u32[]{:S(2)}) %collective-permute-start.44) | collective-permute-done | bytes 589856 | tf_op jit(solution)/shard_map/ppermute | solution.py:82
  184.6 12.7 %collective-permute-done.45.refs_5_ = bf16[2,96,1536]{2,1,0:T(8,128)(2,1)} collective-permute-done((bf16[2,96,1536]{2,1,0:T(8,128)(2,1)}, bf16[2,96,1536]{2,1,0:T(8,128)(2,1)}, u32[]{:S(2)}, u32[]{:S(2)}) %collective-permute-start.45) | collective-permute-done | bytes 589856 | tf_op jit(solution)/shard_map/ppermute | solution.py:82
  207.2 5.6 shared.4
  212.8 6.1 shared.5
  218.8 6.1 shared.6
  225.7 6.4 shared.7
  260.6 6.3 collective-permute-done.7.refs_2_
  267.5 5.8 collective-permute-done.27.refs_3_
  279.6 6.2 collective-permute-done.8.refs_3_
  305.0 9.8 %routed.4 = (f32[576,768]{1,0:T(8,128)}, f32[576,768]{1,0:T(8,128)}, bf16[1,96,1536]{2,1,0:T(8,128)(2,1)}, bf16[1,96,1536]{2,1,0:T(8,128)(2,1)}, bf16[1,96,1536]...) custom-call(s32[12]{0:T(128)} %stack.89.info, ...), custom_call_target="tpu_custom_call" | custom-call | flops 4076863488 | bytes 9437184 | tf_op jit(solution)/shard_map/routed/pallas_call | solution.py:327
  322.1 10.8 %routed.5 = (f32[576,768]{1,0:T(8,128)}, f32[576,768]{1,0:T(8,128)}, bf16[1,96,1536]{2,1,0:T(8,128)(2,1)}, bf16[1,96,1536]{2,1,0:T(8,128)(2,1)}, bf16[1,96,1536]...) custom-call(s32[12]{0:T(128)} %stack.89.info, ...), custom_call_target="tpu_custom_call" | custom-call | flops 4076863488 | bytes 9437184 | tf_op jit(solution)/shard_map/routed/pallas_call | solution.py:327
  346.5 10.8 %routed.6 = (f32[576,768]{1,0:T(8,128)}, f32[576,768]{1,0:T(8,128)}, bf16[1,96,1536]{2,1,0:T(8,128)(2,1)}, bf16[1,96,1536]{2,1,0:T(8,128)(2,1)}, bf16[1,96,1536]...) custom-call(s32[12]{0:T(128)} %stack.89.info, ...), custom_call_target="tpu_custom_call" | custom-call | flops 4076863488 | bytes 9437184 | tf_op jit(solution)/shard_map/routed/pallas_call | solution.py:327
  359.3 6.0 collective-permute-done.32.refs_8_
  371.0 10.3 %routed.7 = (bf16[4,2,144,768]{3,2,1,0:T(8,128)(2,1)}, bf16[1,96,1536]{2,1,0:T(8,128)(2,1)}, bf16[1,96,1536]{2,1,0:T(8,128)(2,1)}, bf16[1,96,1536]{2,1,0:T(8,128...) custom-call(s32[12]{0:T(128)} %stack.89.info, ...), custom_call_target="tpu_custom_call" | custom-call | flops 4076863488 | bytes 9437184 | tf_op jit(solution)/shard_map/routed/pallas_call | solution.py:327
  387.3 7.4 %collective-permute-done.88 = bf16[1,96,1536]{2,1,0:T(8,128)(2,1)S(1)} collective-permute-done((bf16[1,96,1536]{2,1,0:T(8,128)(2,1)}, bf16[1,96,1536]{2,1,0:T(8,128)(2,1)S(1)}, u32[]{:S(2)}, u32[]{:S(2)}) %collective-permute-start.88) | collective-permute-done | bytes 294944 | tf_op jit(solution)/shard_map/ppermute | solution.py:79
  396.9 6.6 collective-permute-done.95
  404.6 6.5 collective-permute-done.102
  416.1 6.1 collective-permute-done.80
  423.4 8.6 %collective-permute-done.87 = bf16[1,96,1536]{2,1,0:T(8,128)(2,1)S(1)} collective-permute-done((bf16[1,96,1536]{2,1,0:T(8,128)(2,1)S(1)}, bf16[1,96,1536]{2,1,0:T(8,128)(2,1)S(1)}, u32[]{:S(2)}, u32[]{:S(2)}) %collective-permute-start.87) | collective-permute-done | bytes 294944 | tf_op jit(solution)/shard_map/ppermute | solution.py:79
  433.3 7.7 %collective-permute-done.94 = bf16[1,96,1536]{2,1,0:T(8,128)(2,1)S(1)} collective-permute-done((bf16[1,96,1536]{2,1,0:T(8,128)(2,1)S(1)}, bf16[1,96,1536]{2,1,0:T(8,128)(2,1)S(1)}, u32[]{:S(2)}, u32[]{:S(2)}) %collective-permute-start.94) | collective-permute-done | bytes 294944 | tf_op jit(solution)/shard_map/ppermute | solution.py:79
  443.6 7.2 %collective-permute-done.101 = bf16[1,96,1536]{2,1,0:T(8,128)(2,1)S(1)} collective-permute-done((bf16[1,96,1536]{2,1,0:T(8,128)(2,1)S(1)}, bf16[1,96,1536]{2,1,0:T(8,128)(2,1)S(1)}, u32[]{:S(2)}, u32[]{:S(2)}) %collective-permute-start.101) | collective-permute-done | bytes 294944 | tf_op jit(solution)/shard_map/ppermute | solution.py:79
  456.1 9.6 %collective-permute-done.83 = bf16[1,96,1536]{2,1,0:T(8,128)(2,1)S(1)} collective-permute-done((bf16[1,96,1536]{2,1,0:T(8,128)(2,1)S(1)}, bf16[1,96,1536]{2,1,0:T(8,128)(2,1)S(1)}, u32[]{:S(2)}, u32[]{:S(2)}) %collective-permute-start.83) | collective-permute-done | bytes 294944 | tf_op jit(solution)/shard_map/ppermute | solution.py:76
  466.9 10.6 %collective-permute-done.90 = bf16[1,96,1536]{2,1,0:T(8,128)(2,1)S(1)} collective-permute-done((bf16[1,96,1536]{2,1,0:T(8,128)(2,1)S(1)}, bf16[1,96,1536]{2,1,0:T(8,128)(2,1)S(1)}, u32[]{:S(2)}, u32[]{:S(2)}) %collective-permute-start.90) | collective-permute-done | bytes 294944 | tf_op jit(solution)/shard_map/ppermute | solution.py:76
  478.3 10.0 %collective-permute-done.97 = bf16[1,96,1536]{2,1,0:T(8,128)(2,1)S(1)} collective-permute-done((bf16[1,96,1536]{2,1,0:T(8,128)(2,1)S(1)}, bf16[1,96,1536]{2,1,0:T(8,128)(2,1)S(1)}, u32[]{:S(2)}, u32[]{:S(2)}) %collective-permute-start.97) | collective-permute-done | bytes 294944 | tf_op jit(solution)/shard_map/ppermute | solution.py:76
  489.2 9.1 %collective-permute-done.104 = bf16[1,96,1536]{2,1,0:T(8,128)(2,1)S(1)} collective-permute-done((bf16[1,96,1536]{2,1,0:T(8,128)(2,1)S(1)}, bf16[1,96,1536]{2,1,0:T(8,128)(2,1)S(1)}, u32[]{:S(2)}, u32[]{:S(2)}) %collective-permute-start.104) | collective-permute-done | bytes 294944 | tf_op jit(solution)/shard_map/ppermute | solution.py:76
  513.9 9.8 %collective-permute-done.91 = bf16[1,96,1536]{2,1,0:T(8,128)(2,1)} collective-permute-done((bf16[1,96,1536]{2,1,0:T(8,128)(2,1)}, bf16[1,96,1536]{2,1,0:T(8,128)(2,1)}, u32[]{:S(2)}, u32[]{:S(2)}) %collective-permute-start.91) | collective-permute-done | bytes 294944 | tf_op jit(solution)/shard_map/ppermute | solution.py:76
  525.0 8.4 %collective-permute-done.98 = bf16[1,96,1536]{2,1,0:T(8,128)(2,1)S(1)} collective-permute-done((bf16[1,96,1536]{2,1,0:T(8,128)(2,1)}, bf16[1,96,1536]{2,1,0:T(8,128)(2,1)S(1)}, u32[]{:S(2)}, u32[]{:S(2)}) %collective-permute-start.98) | collective-permute-done | bytes 294944 | tf_op jit(solution)/shard_map/ppermute | solution.py:76
  546.7 8.4 %middle.1 = (bf16[256,768]{1,0:T(8,128)(2,1)}, f32[256,768]{1,0:T(8,128)}, f32[2,4,768]{2,1,0:T(4,128)}, f32[128,768]{1,0:T(8,128)}, bf16[2,8,96,192]{3,2,1,0:T(...) custom-call(s32[12]{0:T(128)} %stack.89.info, bf16[4,2,144,768]{3,2,1,0:T(8,128)(2,1)} %copy-done.4, ...), custom_call_target="tpu_custom_call" | custom-call | tf_op jit(solution)/shard_map/middle/pallas_call | solution.py:650
  564.6 5.4 all-to-all-done.5
  571.1 9.3 %attend_back.1 = bf16[4,256,576]{2,1,0:T(8,128)(2,1)} custom-call(bf16[4,256,576]{2,1,0:T(8,128)(2,1)} %copy.105.projected, bf16[4,256,192]{2,1,0:T(8,128)(2,1)} %copy.121.grad_mixed), custom_call_target="tpu_custom_call" | custom-call | tf_op jit(solution)/shard_map/attend_back/pallas_call | solution.py:681
  594.0 8.9 %all-to-all-done.6 = bf16[4,256,576]{1,2,0:T(8,128)(2,1)S(1)} async-done(((bf16[4,256,576]{1,2,0:T(8,128)(2,1)}), bf16[4,256,576]{1,2,0:T(8,128)(2,1)S(1)}, u32[]{:S(2)}, u32[]{:S(2)}) %all-to-all-start.6) | async-done | bytes 1179680 | tf_op jit(solution)/shard_map/all_to_all | solution.py:689
  604.4 5.9 qkv_grad.1
  614.3 5.7 collective-permute-done.58
  645.7 10.7 %collective-permute-done.51 = bf16[8,96,576]{2,1,0:T(8,128)(2,1)} collective-permute-done((bf16[8,96,576]{2,1,0:T(8,128)(2,1)S(1)}, bf16[8,96,576]{2,1,0:T(8,128)(2,1)}, u32[]{:S(2)}, u32[]{:S(2)}) %collective-permute-start.51) | collective-permute-done | bytes 884768 | tf_op jit(solution)/shard_map/ppermute | solution.py:82
  662.6 6.8 collective-permute-done.52
  670.8 7.2 %collective-permute-done.53 = bf16[96,576]{1,0:T(8,128)(2,1)S(1)} collective-permute-done((bf16[96,576]{1,0:T(8,128)(2,1)S(1)}, bf16[96,576]{1,0:T(8,128)(2,1)S(1)}, u32[]{:S(2)}, u32[]{:S(2)}) %collective-permute-start.53) | collective-permute-done | bytes 110624 | tf_op jit(solution)/shard_map/ppermute | solution.py:76
  686.7 6.1 collective-permute-done.55
  (518 shorter events, 277.1 us)
Async XLA Ops:
  32.5 27.1 %collective-permute-start.4 = (bf16[1,8,96,768]{3,2,1,0:T(8,128)(2,1)S(1)}, bf16[1,8,96,768]{3,2,1,0:T(8,128)(2,1)}, u32[]{:S(2)}, u32[]{:S(2)}) collective-permute-start(bf16[1,8,96,768]{3,2,1,0:T(8,128)(2,1)S(1)} %bitcast.192), channel_id=1, source_target_pairs={{0,2},{1,3},{2,0},{3,1},{4,6},{5,7},{6,4},{7,5},{8,10},{9,11},{10,... | collective-permute-start | bytes 3538952 | tf_op jit(solution)/shard_map/ppermute | solution.py:82
  34.5 38.6 %collective-permute-start.34 = (bf16[96,1536]{1,0:T(8,128)(2,1)S(1)}, bf16[96,1536]{1,0:T(8,128)(2,1)}, u32[]{:S(2)}, u32[]{:S(2)}) collective-permute-start(bf16[96,1536]{1,0:T(8,128)(2,1)S(1)} %bitcast.209), channel_id=1, source_target_pairs={{0,4},{4,0},{8,12},{12,8},{16,20},{20,16},{24,28},{28,24},{1,5},{5... | collective-permute-start | bytes 884744 | tf_op jit(solution)/shard_map/ppermute | solution.py:79
  61.5 64.6 %collective-permute-start.5 = (bf16[2,8,96,768]{3,2,1,0:T(8,128)(2,1)S(1)}, bf16[2,8,96,768]{3,2,1,0:T(8,128)(2,1)}, u32[]{:S(2)}, u32[]{:S(2)}) collective-permute-start(bf16[2,8,96,768]{3,2,1,0:T(8,128)(2,1)S(1)} %pad_maximum_fusion.refs_0_), channel_id=1, source_target_pairs={{0,1},{1,0},{2,3},{3,2},{4,5},{5,4},{6,7},{7,6},{8,9},{9,8},{10,11... | collective-permute-start | bytes 7077896 | tf_op jit(solution)/shard_map/ppermute | solution.py:82
  91.3 33.3 %all-to-all-start = ((f32[32,1,2400]{2,1,0:T(1,128)}), f32[32,1,2400]{2,1,0:T(1,128)S(1)}, u32[]{:S(2)}, u32[]{:S(2)}) async-start(f32[32,1,2400]{2,1,0:T(1,128)} %all_to_all.30), calls=%async_computation | async-start | bytes 622592 | tf_op jit(solution)/shard_map/all_to_all | solution.py:520
  97.4 48.0 %collective-permute-start.38 = (bf16[2,96,1536]{2,1,0:T(8,128)(2,1)}, bf16[2,96,1536]{2,1,0:T(8,128)(2,1)}, u32[]{:S(2)}, u32[]{:S(2)}) collective-permute-start(bf16[2,96,1536]{2,1,0:T(8,128)(2,1)} %pad_maximum_fusion.2.refs_0_), channel_id=1, source_target_pairs={{0,1},{1,0},{2,3},{3,2},{4,5},{5,4},{6,7},{7,6},{8,9},{9,8},{10,11... | collective-permute-start | bytes 1769480 | tf_op jit(solution)/shard_map/ppermute | solution.py:82
  97.7 47.8 %collective-permute-start.42 = (bf16[2,96,1536]{2,1,0:T(8,128)(2,1)}, bf16[2,96,1536]{2,1,0:T(8,128)(2,1)}, u32[]{:S(2)}, u32[]{:S(2)}) collective-permute-start(bf16[2,96,1536]{2,1,0:T(8,128)(2,1)} %pad_maximum_fusion.2.refs_0_), channel_id=1, source_target_pairs={{0,2},{1,3},{2,0},{3,1},{4,6},{5,7},{6,4},{7,5},{8,10},{9,11},{10,... | collective-permute-start | bytes 1769480 | tf_op jit(solution)/shard_map/ppermute | solution.py:82
  106.6 39.3 %collective-permute-start.37 = (bf16[2,96,1536]{2,1,0:T(8,128)(2,1)}, bf16[2,96,1536]{2,1,0:T(8,128)(2,1)}, u32[]{:S(2)}, u32[]{:S(2)}) collective-permute-start(bf16[2,96,1536]{2,1,0:T(8,128)(2,1)} %collective-permute-done.36.refs_2_), channel_id=1, source_target_pairs={{0,8},{4,12},{8,16},{12,20},{16,24},{20,28},{24,0},{28,4},{1,9},{5... | collective-permute-start | bytes 1769480 | tf_op jit(solution)/shard_map/ppermute | solution.py:76
  143.0 29.7 %collective-permute-start.39 = (bf16[2,96,1536]{2,1,0:T(8,128)(2,1)}, bf16[2,96,1536]{2,1,0:T(8,128)(2,1)}, u32[]{:S(2)}, u32[]{:S(2)}) collective-permute-start(bf16[2,96,1536]{2,1,0:T(8,128)(2,1)} %collective-permute-done.35.refs_1_), channel_id=1, source_target_pairs={{0,1},{1,0},{2,3},{3,2},{4,5},{5,4},{6,7},{7,6},{8,9},{9,8},{10,11... | collective-permute-start | bytes 1769480 | tf_op jit(solution)/shard_map/ppermute | solution.py:82
  143.7 30.9 %collective-permute-start.43 = (bf16[2,96,1536]{2,1,0:T(8,128)(2,1)}, bf16[2,96,1536]{2,1,0:T(8,128)(2,1)S(1)}, u32[]{:S(2)}, u32[]{:S(2)}) collective-permute-start(bf16[2,96,1536]{2,1,0:T(8,128)(2,1)} %collective-permute-done.35.refs_1_), channel_id=1, source_target_pairs={{0,2},{1,3},{2,0},{3,1},{4,6},{5,7},{6,4},{7,5},{8,10},{9,11},{10,... | collective-permute-start | bytes 1769480 | tf_op jit(solution)/shard_map/ppermute | solution.py:82
  145.4 29.2 %collective-permute-start.40 = (bf16[2,96,1536]{2,1,0:T(8,128)(2,1)}, bf16[2,96,1536]{2,1,0:T(8,128)(2,1)}, u32[]{:S(2)}, u32[]{:S(2)}) collective-permute-start(bf16[2,96,1536]{2,1,0:T(8,128)(2,1)} %collective-permute-done.36.refs_2_), channel_id=1, source_target_pairs={{0,1},{1,0},{2,3},{3,2},{4,5},{5,4},{6,7},{7,6},{8,9},{9,8},{10,11... | collective-permute-start | bytes 1769480 | tf_op jit(solution)/shard_map/ppermute | solution.py:82
  145.5 39.1 %collective-permute-start.44 = (bf16[2,96,1536]{2,1,0:T(8,128)(2,1)}, bf16[2,96,1536]{2,1,0:T(8,128)(2,1)S(1)}, u32[]{:S(2)}, u32[]{:S(2)}) collective-permute-start(bf16[2,96,1536]{2,1,0:T(8,128)(2,1)} %collective-permute-done.36.refs_2_), channel_id=1, source_target_pairs={{0,2},{1,3},{2,0},{3,1},{4,6},{5,7},{6,4},{7,5},{8,10},{9,11},{10,... | collective-permute-start | bytes 1769480 | tf_op jit(solution)/shard_map/ppermute | solution.py:82
  145.8 51.5 %collective-permute-start.45 = (bf16[2,96,1536]{2,1,0:T(8,128)(2,1)}, bf16[2,96,1536]{2,1,0:T(8,128)(2,1)}, u32[]{:S(2)}, u32[]{:S(2)}) collective-permute-start(bf16[2,96,1536]{2,1,0:T(8,128)(2,1)} %collective-permute-done.37.refs_3_), channel_id=1, source_target_pairs={{0,2},{1,3},{2,0},{3,1},{4,6},{5,7},{6,4},{7,5},{8,10},{9,11},{10,... | collective-permute-start | bytes 1769480 | tf_op jit(solution)/shard_map/ppermute | solution.py:82
  169.0 31.9 %all-to-all-start.2 = ((bf16[4,256,192]{1,2,0:T(8,128)(2,1)}), bf16[4,256,192]{1,2,0:T(8,128)(2,1)S(1)}, u32[]{:S(2)}, u32[]{:S(2)}) async-start(bf16[4,256,192]{1,2,0:T(8,128)(2,1)} %copy.106), calls=%async_computation.2 | async-start | bytes 786432 | tf_op jit(solution)/shard_map/all_to_all | solution.py:586
  172.7 40.1 %collective-permute-start.41 = (bf16[2,96,1536]{2,1,0:T(8,128)(2,1)}, bf16[2,96,1536]{2,1,0:T(8,128)(2,1)}, u32[]{:S(2)}, u32[]{:S(2)}) collective-permute-start(bf16[2,96,1536]{2,1,0:T(8,128)(2,1)} %collective-permute-done.37.refs_3_), channel_id=1, source_target_pairs={{0,1},{1,0},{2,3},{3,2},{4,5},{5,4},{6,7},{7,6},{8,9},{9,8},{10,11... | collective-permute-start | bytes 1769480 | tf_op jit(solution)/shard_map/ppermute | solution.py:82
  174.6 50.3 %collective-permute-start.46 = (bf16[2,96,1536]{2,1,0:T(8,128)(2,1)}, bf16[2,96,1536]{2,1,0:T(8,128)(2,1)S(1)}, u32[]{:S(2)}, u32[]{:S(2)}) collective-permute-start(bf16[2,96,1536]{2,1,0:T(8,128)(2,1)} %collective-permute-done.42.refs_2_), channel_id=1, source_target_pairs={{0,1},{1,0},{2,3},{3,2},{4,5},{5,4},{6,7},{7,6},{8,9},{9,8},{10,11... | collective-permute-start | bytes 1769480 | tf_op jit(solution)/shard_map/ppermute | solution.py:82
  174.6 50.2 %collective-permute-start.47 = (bf16[2,96,1536]{2,1,0:T(8,128)(2,1)S(1)}, bf16[2,96,1536]{2,1,0:T(8,128)(2,1)}, u32[]{:S(2)}, u32[]{:S(2)}) collective-permute-start(bf16[2,96,1536]{2,1,0:T(8,128)(2,1)S(1)} %collective-permute-done.43.refs_3_), channel_id=1, source_target_pairs={{0,1},{1,0},{2,3},{3,2},{4,5},{5,4},{6,7},{7,6},{8,9},{9,8},{10,11... | collective-permute-start | bytes 1769480 | tf_op jit(solution)/shard_map/ppermute | solution.py:82
  184.6 40.3 %collective-permute-start.48 = (bf16[2,96,1536]{2,1,0:T(8,128)(2,1)S(1)}, bf16[2,96,1536]{2,1,0:T(8,128)(2,1)}, u32[]{:S(2)}, u32[]{:S(2)}) collective-permute-start(bf16[2,96,1536]{2,1,0:T(8,128)(2,1)S(1)} %collective-permute-done.44.refs_4_), channel_id=1, source_target_pairs={{0,1},{1,0},{2,3},{3,2},{4,5},{5,4},{6,7},{7,6},{8,9},{9,8},{10,11... | collective-permute-start | bytes 1769480 | tf_op jit(solution)/shard_map/ppermute | solution.py:82
  197.3 27.6 %collective-permute-start.49 = (bf16[2,96,1536]{2,1,0:T(8,128)(2,1)}, bf16[2,96,1536]{2,1,0:T(8,128)(2,1)}, u32[]{:S(2)}, u32[]{:S(2)}) collective-permute-start(bf16[2,96,1536]{2,1,0:T(8,128)(2,1)} %collective-permute-done.45.refs_5_), channel_id=1, source_target_pairs={{0,1},{1,0},{2,3},{3,2},{4,5},{5,4},{6,7},{7,6},{8,9},{9,8},{10,11... | collective-permute-start | bytes 1769480 | tf_op jit(solution)/shard_map/ppermute | solution.py:82
  239.4 64.4 %all-to-all-start.3 = ((bf16[4,2,144,768]{3,2,1,0:T(8,128)(2,1)}), bf16[4,2,144,768]{3,2,1,0:T(8,128)(2,1)S(1)}, u32[]{:S(2)}, u32[]{:S(2)}) async-start(bf16[4,2,144,768]{3,2,1,0:T(8,128)(2,1)} %get-tuple-element.99), calls=%async_computation.3 | async-start | bytes 3538944 | tf_op jit(solution)/shard_map/all_to_all | solution.py:603
  253.9 32.9 %collective-permute-start.71 = (bf16[2,96,1536]{2,1,0:T(8,128)(2,1)S(1)}, bf16[2,96,1536]{2,1,0:T(8,128)(2,1)S(1)}, u32[]{:S(2)}, u32[]{:S(2)}) collective-permute-start(bf16[2,96,1536]{2,1,0:T(8,128)(2,1)S(1)} %copy-done.54), channel_id=1, source_target_pairs={{0,1},{1,0},{2,3},{3,2},{4,5},{5,4},{6,7},{7,6},{8,9},{9,8},{10,11... | collective-permute-start | bytes 1769480 | tf_op jit(solution)/shard_map/ppermute | solution.py:82
  253.9 32.9 %collective-permute-start.73 = (bf16[2,96,1536]{2,1,0:T(8,128)(2,1)S(1)}, bf16[2,96,1536]{2,1,0:T(8,128)(2,1)S(1)}, u32[]{:S(2)}, u32[]{:S(2)}) collective-permute-start(bf16[2,96,1536]{2,1,0:T(8,128)(2,1)S(1)} %add_convert_fusion.3), channel_id=1, source_target_pairs={{0,2},{1,3},{2,0},{3,1},{4,6},{5,7},{6,4},{7,5},{8,10},{9,11},{10,... | collective-permute-start | bytes 1769480 | tf_op jit(solution)/shard_map/ppermute | solution.py:82
  289.0 25.8 %collective-permute-start.17 = (bf16[1,96,1536]{2,1,0:T(8,128)(2,1)}, bf16[1,96,1536]{2,1,0:T(8,128)(2,1)}, u32[]{:S(2)}, u32[]{:S(2)}) collective-permute-start(bf16[1,96,1536]{2,1,0:T(8,128)(2,1)} %collective-permute-done.13.refs_3_), channel_id=1, source_target_pairs={{0,4},{4,0},{8,12},{12,8},{16,20},{20,16},{24,28},{28,24},{1,5},{5... | collective-permute-start | bytes 884744 | tf_op jit(solution)/shard_map/ppermute | solution.py:79
  292.3 23.7 %collective-permute-start.28 = (bf16[1,96,1536]{2,1,0:T(8,128)(2,1)}, bf16[1,96,1536]{2,1,0:T(8,128)(2,1)}, u32[]{:S(2)}, u32[]{:S(2)}) collective-permute-start(bf16[1,96,1536]{2,1,0:T(8,128)(2,1)} %collective-permute-done.27.refs_3_), channel_id=1, source_target_pairs={{0,8},{4,12},{8,16},{12,20},{16,24},{20,28},{24,0},{28,4},{1,9},{5... | collective-permute-start | bytes 884744 | tf_op jit(solution)/shard_map/ppermute | solution.py:76
  316.9 23.1 %collective-permute-start.25 = (bf16[1,96,1536]{2,1,0:T(8,128)(2,1)}, bf16[1,96,1536]{2,1,0:T(8,128)(2,1)S(1)}, u32[]{:S(2)}, u32[]{:S(2)}) collective-permute-start(bf16[1,96,1536]{2,1,0:T(8,128)(2,1)} %collective-permute-done.21.refs_4_), channel_id=1, source_target_pairs={{0,4},{4,0},{8,12},{12,8},{16,20},{20,16},{24,28},{28,24},{1,5},{5... | collective-permute-start | bytes 884744 | tf_op jit(solution)/shard_map/ppermute | solution.py:79
  318.0 22.9 %collective-permute-start.29 = (bf16[1,96,1536]{2,1,0:T(8,128)(2,1)}, bf16[1,96,1536]{2,1,0:T(8,128)(2,1)S(1)}, u32[]{:S(2)}, u32[]{:S(2)}) collective-permute-start(bf16[1,96,1536]{2,1,0:T(8,128)(2,1)} %collective-permute-done.28.refs_4_), channel_id=1, source_target_pairs={{0,8},{4,12},{8,16},{12,20},{16,24},{20,28},{24,0},{28,4},{1,9},{5... | collective-permute-start | bytes 884744 | tf_op jit(solution)/shard_map/ppermute | solution.py:76
  321.2 25.3 %collective-permute-start.26 = (bf16[1,96,1536]{2,1,0:T(8,128)(2,1)}, bf16[1,96,1536]{2,1,0:T(8,128)(2,1)}, u32[]{:S(2)}, u32[]{:S(2)}) collective-permute-start(bf16[1,96,1536]{2,1,0:T(8,128)(2,1)} %collective-permute-done.22.refs_5_), channel_id=1, source_target_pairs={{0,4},{4,0},{8,12},{12,8},{16,20},{20,16},{24,28},{28,24},{1,5},{5... | collective-permute-start | bytes 884744 | tf_op jit(solution)/shard_map/ppermute | solution.py:79
  332.9 24.4 %collective-permute-start.30 = (bf16[1,96,1536]{2,1,0:T(8,128)(2,1)S(1)}, bf16[1,96,1536]{2,1,0:T(8,128)(2,1)S(1)}, u32[]{:S(2)}, u32[]{:S(2)}) collective-permute-start(bf16[1,96,1536]{2,1,0:T(8,128)(2,1)S(1)} %broadcast_in_dim_reshape.16.refs_2_), channel_id=1, source_target_pairs={{0,4},{4,0},{8,12},{12,8},{16,20},{20,16},{24,28},{28,24},{1,5},{5... | collective-permute-start | bytes 884744 | tf_op jit(solution)/shard_map/ppermute | solution.py:79
  334.1 24.9 %collective-permute-start.31 = (bf16[1,96,1536]{2,1,0:T(8,128)(2,1)}, bf16[1,96,1536]{2,1,0:T(8,128)(2,1)S(1)}, u32[]{:S(2)}, u32[]{:S(2)}) collective-permute-start(bf16[1,96,1536]{2,1,0:T(8,128)(2,1)} %collective-permute-done.27.refs_3_), channel_id=1, source_target_pairs={{0,4},{4,0},{8,12},{12,8},{16,20},{20,16},{24,28},{28,24},{1,5},{5... | collective-permute-start | bytes 884744 | tf_op jit(solution)/shard_map/ppermute | solution.py:79
  340.0 25.3 %collective-permute-start.32 = (bf16[1,96,1536]{2,1,0:T(8,128)(2,1)}, bf16[1,96,1536]{2,1,0:T(8,128)(2,1)S(1)}, u32[]{:S(2)}, u32[]{:S(2)}) collective-permute-start(bf16[1,96,1536]{2,1,0:T(8,128)(2,1)} %collective-permute-done.28.refs_4_), channel_id=1, source_target_pairs={{0,4},{4,0},{8,12},{12,8},{16,20},{20,16},{24,28},{28,24},{1,5},{5... | collective-permute-start | bytes 884744 | tf_op jit(solution)/shard_map/ppermute | solution.py:79
  341.0 29.1 %collective-permute-start.33 = (bf16[1,96,1536]{2,1,0:T(8,128)(2,1)S(1)}, bf16[1,96,1536]{2,1,0:T(8,128)(2,1)}, u32[]{:S(2)}, u32[]{:S(2)}) collective-permute-start(bf16[1,96,1536]{2,1,0:T(8,128)(2,1)S(1)} %collective-permute-done.29.refs_5_), channel_id=1, source_target_pairs={{0,4},{4,0},{8,12},{12,8},{16,20},{20,16},{24,28},{28,24},{1,5},{5... | collective-permute-start | bytes 884744 | tf_op jit(solution)/shard_map/ppermute | solution.py:79
  346.4 65.7 %collective-permute-start.68 = (bf16[2,96,1536]{2,1,0:T(8,128)(2,1)}, bf16[2,96,1536]{2,1,0:T(8,128)(2,1)}, u32[]{:S(2)}, u32[]{:S(2)}) collective-permute-start(bf16[2,96,1536]{2,1,0:T(8,128)(2,1)} %get-tuple-element.143), channel_id=1, source_target_pairs={{0,1},{1,0},{2,3},{3,2},{4,5},{5,4},{6,7},{7,6},{8,9},{9,8},{10,11... | collective-permute-start | bytes 1769480 | tf_op jit(solution)/shard_map/ppermute | solution.py:82
  357.3 142.5 %collective-permute-start.65 = (bf16[2,96,1536]{2,1,0:T(8,128)(2,1)}, bf16[2,96,1536]{2,1,0:T(8,128)(2,1)}, u32[]{:S(2)}, u32[]{:S(2)}) collective-permute-start(bf16[2,96,1536]{2,1,0:T(8,128)(2,1)} %get-tuple-element.139), channel_id=1, source_target_pairs={{0,1},{1,0},{2,3},{3,2},{4,5},{5,4},{6,7},{7,6},{8,9},{9,8},{10,11... | collective-permute-start | bytes 1769480 | tf_op jit(solution)/shard_map/ppermute | solution.py:82
  359.0 54.3 %collective-permute-start.70 = (bf16[2,96,1536]{2,1,0:T(8,128)(2,1)S(1)}, bf16[2,96,1536]{2,1,0:T(8,128)(2,1)}, u32[]{:S(2)}, u32[]{:S(2)}) collective-permute-start(bf16[2,96,1536]{2,1,0:T(8,128)(2,1)S(1)} %add_convert_fusion.4), channel_id=1, source_target_pairs={{0,2},{1,3},{2,0},{3,1},{4,6},{5,7},{6,4},{7,5},{8,10},{9,11},{10,... | collective-permute-start | bytes 1769480 | tf_op jit(solution)/shard_map/ppermute | solution.py:82
  365.3 49.0 %collective-permute-start.74 = (bf16[2,96,1536]{2,1,0:T(8,128)(2,1)}, bf16[2,96,1536]{2,1,0:T(8,128)(2,1)}, u32[]{:S(2)}, u32[]{:S(2)}) collective-permute-start(bf16[2,96,1536]{2,1,0:T(8,128)(2,1)} %add_convert_fusion.2), channel_id=1, source_target_pairs={{0,8},{4,12},{8,16},{12,20},{16,24},{20,28},{24,0},{28,4},{1,9},{5... | collective-permute-start | bytes 1769480 | tf_op jit(solution)/shard_map/ppermute | solution.py:76
  381.2 164.2 %all-to-all-start.4 = ((bf16[4,2,144,768]{3,2,1,0:T(8,128)(2,1)}), bf16[4,2,144,768]{3,2,1,0:T(8,128)(2,1)S(1)}, u32[]{:S(2)}, u32[]{:S(2)}) async-start(bf16[4,2,144,768]{3,2,1,0:T(8,128)(2,1)} %get-tuple-element.106), calls=%async_computation.4 | async-start | bytes 3538944 | tf_op jit(solution)/shard_map/all_to_all | solution.py:621
  411.1 89.7 %collective-permute-start.67 = (bf16[2,96,1536]{2,1,0:T(8,128)(2,1)S(1)}, bf16[2,96,1536]{2,1,0:T(8,128)(2,1)S(1)}, u32[]{:S(2)}, u32[]{:S(2)}) collective-permute-start(bf16[2,96,1536]{2,1,0:T(8,128)(2,1)S(1)} %add_convert_fusion.5), channel_id=1, source_target_pairs={{0,2},{1,3},{2,0},{3,1},{4,6},{5,7},{6,4},{7,5},{8,10},{9,11},{10,... | collective-permute-start | bytes 1769480 | tf_op jit(solution)/shard_map/ppermute | solution.py:82
  413.3 41.7 %collective-permute-start.79 = (bf16[1,96,1536]{2,1,0:T(8,128)(2,1)S(1)}, bf16[1,96,1536]{2,1,0:T(8,128)(2,1)S(1)}, u32[]{:S(2)}, u32[]{:S(2)}) collective-permute-start(bf16[1,96,1536]{2,1,0:T(8,128)(2,1)S(1)} %copy-done.60), channel_id=1, source_target_pairs={{0,4},{4,0},{8,12},{12,8},{16,20},{20,16},{24,28},{28,24},{1,5},{5... | collective-permute-start | bytes 884744 | tf_op jit(solution)/shard_map/ppermute | solution.py:79
  455.1 23.2 %collective-permute-start.93 = (bf16[1,96,1536]{2,1,0:T(8,128)(2,1)S(1)}, bf16[1,96,1536]{2,1,0:T(8,128)(2,1)S(1)}, u32[]{:S(2)}, u32[]{:S(2)}) collective-permute-start(bf16[1,96,1536]{2,1,0:T(8,128)(2,1)S(1)} %copy-done.62), channel_id=1, source_target_pairs={{0,4},{4,0},{8,12},{12,8},{16,20},{20,16},{24,28},{28,24},{1,5},{5... | collective-permute-start | bytes 884744 | tf_op jit(solution)/shard_map/ppermute | solution.py:79
  465.9 23.3 %collective-permute-start.100 = (bf16[1,96,1536]{2,1,0:T(8,128)(2,1)S(1)}, bf16[1,96,1536]{2,1,0:T(8,128)(2,1)S(1)}, u32[]{:S(2)}, u32[]{:S(2)}) collective-permute-start(bf16[1,96,1536]{2,1,0:T(8,128)(2,1)S(1)} %copy-done.66), channel_id=1, source_target_pairs={{0,4},{4,0},{8,12},{12,8},{16,20},{20,16},{24,28},{28,24},{1,5},{5... | collective-permute-start | bytes 884744 | tf_op jit(solution)/shard_map/ppermute | solution.py:79
  478.3 23.6 %collective-permute-start.75 = (bf16[2,96,1536]{2,1,0:T(8,128)(2,1)S(1)}, bf16[2,96,1536]{2,1,0:T(8,128)(2,1)S(1)}, u32[]{:S(2)}, u32[]{:S(2)}) collective-permute-start(bf16[2,96,1536]{2,1,0:T(8,128)(2,1)S(1)} %add_convert_fusion.1), channel_id=1, source_target_pairs={{0,8},{4,12},{8,16},{12,20},{16,24},{20,28},{24,0},{28,4},{1,9},{5... | collective-permute-start | bytes 1769480 | tf_op jit(solution)/shard_map/ppermute | solution.py:76
  489.2 102.0 %collective-permute-start.62 = (bf16[2,96,1536]{2,1,0:T(8,128)(2,1)}, bf16[2,96,1536]{2,1,0:T(8,128)(2,1)}, u32[]{:S(2)}, u32[]{:S(2)}) collective-permute-start(bf16[2,96,1536]{2,1,0:T(8,128)(2,1)} %get-tuple-element.135), channel_id=1, source_target_pairs={{0,1},{1,0},{2,3},{3,2},{4,5},{5,4},{6,7},{7,6},{8,9},{9,8},{10,11... | collective-permute-start | bytes 1769480 | tf_op jit(solution)/shard_map/ppermute | solution.py:82
  498.2 93.0 %collective-permute-start.64 = (bf16[2,96,1536]{2,1,0:T(8,128)(2,1)}, bf16[2,96,1536]{2,1,0:T(8,128)(2,1)}, u32[]{:S(2)}, u32[]{:S(2)}) collective-permute-start(bf16[2,96,1536]{2,1,0:T(8,128)(2,1)} %add_convert_fusion.6), channel_id=1, source_target_pairs={{0,2},{1,3},{2,0},{3,1},{4,6},{5,7},{6,4},{7,5},{8,10},{9,11},{10,... | collective-permute-start | bytes 1769480 | tf_op jit(solution)/shard_map/ppermute | solution.py:82
  513.0 28.5 %collective-permute-start.99 = (bf16[1,96,1536]{2,1,0:T(8,128)(2,1)}, bf16[1,96,1536]{2,1,0:T(8,128)(2,1)}, u32[]{:S(2)}, u32[]{:S(2)}) collective-permute-start(bf16[1,96,1536]{2,1,0:T(8,128)(2,1)} %get-tuple-element.175), channel_id=1, source_target_pairs={{0,4},{4,0},{8,12},{12,8},{16,20},{20,16},{24,28},{28,24},{1,5},{5... | collective-permute-start | bytes 884744 | tf_op jit(solution)/shard_map/ppermute | solution.py:79
  533.5 57.7 %collective-permute-start.76 = (bf16[2,96,1536]{2,1,0:T(8,128)(2,1)}, bf16[2,96,1536]{2,1,0:T(8,128)(2,1)}, u32[]{:S(2)}, u32[]{:S(2)}) collective-permute-start(bf16[2,96,1536]{2,1,0:T(8,128)(2,1)} %add_convert_fusion), channel_id=1, source_target_pairs={{0,8},{4,12},{8,16},{12,20},{16,24},{20,28},{24,0},{28,4},{1,9},{5... | collective-permute-start | bytes 1769480 | tf_op jit(solution)/shard_map/ppermute | solution.py:76
  555.1 31.6 %collective-permute-start.56 = (bf16[2,8,96,192]{3,2,1,0:T(8,128)(2,1)}, bf16[2,8,96,192]{3,2,1,0:T(8,128)(2,1)S(1)}, u32[]{:S(2)}, u32[]{:S(2)}) collective-permute-start(bf16[2,8,96,192]{3,2,1,0:T(8,128)(2,1)} %get-tuple-element.133), channel_id=1, source_target_pairs={{0,1},{1,0},{2,3},{3,2},{4,5},{5,4},{6,7},{7,6},{8,9},{9,8},{10,11... | collective-permute-start | bytes 1769480 | tf_op jit(solution)/shard_map/ppermute | solution.py:82
  589.2 21.8 %collective-permute-start.57 = (bf16[8,96,192]{2,1,0:T(8,128)(2,1)S(1)}, bf16[8,96,192]{2,1,0:T(8,128)(2,1)}, u32[]{:S(2)}, u32[]{:S(2)}) collective-permute-start(bf16[8,96,192]{2,1,0:T(8,128)(2,1)S(1)} %fusion.4), channel_id=1, source_target_pairs={{0,2},{1,3},{2,0},{3,1},{4,6},{5,7},{6,4},{7,5},{8,10},{9,11},{10,... | collective-permute-start | bytes 884744 | tf_op jit(solution)/shard_map/ppermute | solution.py:82
  631.0 25.3 %collective-permute-start.51 = (bf16[8,96,576]{2,1,0:T(8,128)(2,1)S(1)}, bf16[8,96,576]{2,1,0:T(8,128)(2,1)}, u32[]{:S(2)}, u32[]{:S(2)}) collective-permute-start(bf16[8,96,576]{2,1,0:T(8,128)(2,1)S(1)} %fusion.1), channel_id=1, source_target_pairs={{0,2},{1,3},{2,0},{3,1},{4,6},{5,7},{6,4},{7,5},{8,10},{9,11},{10,... | collective-permute-start | bytes 2654216 | tf_op jit(solution)/shard_map/ppermute | solution.py:82
  632.9 28.2 %collective-permute-start.61 = (bf16[96,192]{1,0:T(8,128)(2,1)S(1)}, bf16[96,192]{1,0:T(8,128)(2,1)S(1)}, u32[]{:S(2)}, u32[]{:S(2)}) collective-permute-start(bf16[96,192]{1,0:T(8,128)(2,1)S(1)} %fusion.18), channel_id=1, source_target_pairs={{0,8},{4,12},{8,16},{12,20},{16,24},{20,28},{24,0},{28,4},{1,9},{5... | collective-permute-start | bytes 110600 | tf_op jit(solution)/shard_map/ppermute | solution.py:76
  (153 other events, 2037.2 us)
